TPU v7x, 32 devices: a whole 2x2x4 slice. The times are simulated.
32 devices in a mesh: dp: 4 (over x, core), wide: 4 (over z), row: 2 (over y).
Axes of the slice: x: 2, y: 2, z: 4, core: 2. Of those that a mesh axis runs over, the one named last changes fastest.
Arguments:
- patches: bfloat16 [64, 24, 24, 1024], P(('dp', 'wide'), 'row'), may hold values from -6 to 6
- grid_sizes: int32 [64], P(('dp', 'wide')), may hold values from 16 to 24, as said below
- conv_in: bfloat16 [2, 1024, 1024], replicated, may hold values from -0.1875 to 0.1875
- conv_out: bfloat16 [2, 1024, 1024], replicated, may hold values from -0.1875 to 0.1875
- depth_taps: bfloat16 [2, 9, 1024], replicated, may hold values from -2 to 2
- norm_gain: float32 [2, 3, 1024], replicated, may hold values from 0.1 to 1.9
- norm_bias: float32 [2, 3, 1024], replicated, may hold values from -3 to 3
- read_in: bfloat16 [1024, 4096], P(None, 'wide'), may hold values from -0.1875 to 0.1875
- read_bias: float32 [2, 4096], P(None, 'wide'), may hold values from -3 to 3
- read_out: bfloat16 [4096, 4096], P('wide'), may hold values from -0.125 to 0.125
- cotangent: bfloat16 [64, 12, 12, 4096], P('dp', 'row', None, 'wide'), may hold values from -6 to 6
Outputs:
- tokens: bfloat16 [64, 12, 12, 4096], P('dp', 'row', None, 'wide')
- patch_grad: bfloat16 [64, 24, 24, 1024], P(('dp', 'wide'), 'row')
- grad_conv_in: float32 [2, 1024, 1024], P(None, None, ('dp', 'wide'))
- grad_conv_out: float32 [2, 1024, 1024], P(None, None, ('dp', 'wide'))
- grad_taps: float32 [2, 9, 1024], P(None, None, ('dp', 'wide'))
- grad_gain: float32 [2, 3, 1024], P(None, None, ('dp', 'wide'))
- grad_bias: float32 [2, 3, 1024], P(None, None, ('dp', 'wide'))
- grad_read_in: float32 [1024, 4096], P(None, 'wide')
- grad_read_bias: float32 [2, 4096], P(None, 'wide')
- grad_read_out: float32 [4096, 4096], P('wide')
Inputs may be any that keep to these rules, and one draw needn't show every extreme that they name: `grid_sizes`: each entry is 16 or 24; exactly one of the 64 grids has side 16.
All inputs are finite; a program needn't handle non-finite values.
Results may differ from a plain program's by a relative error of at most 0.02.
Values may be sent and summed in bfloat16 or wider, within the bound.
A program may use at most 256 MiB of HBM per device.

v0:
```python
from functools import partial

import jax
import jax.numpy as jnp
from jax import lax
from jax.sharding import PartitionSpec as P

POOL = 12


eps_norm = 1e-06
exact_mode = lax.Precision.HIGHEST


def extended(cells, sides, width):
    for axis, dim in sides:
        count = lax.axis_size(axis)
        ends = count - 1
        head = lax.slice_in_dim(cells, 0, width, axis=dim)
        tail = lax.slice_in_dim(cells, cells.shape[dim] - width, cells.shape[dim], axis=dim)
        cells = jnp.concatenate(
            [
                lax.ppermute(tail, axis, [(i, (i + 1) % count) for i in range(ends)]),
                cells,
                lax.ppermute(head, axis, [((i + 1) % count, i) for i in range(ends)]),
            ],
            axis=dim,
        )
    return cells


def layer_norm(values, gain_row, bias_row):
    centre = jnp.mean(values, axis=-1, keepdims=True)
    centred = values - centre
    variance = jnp.mean(centred * centred, axis=-1, keepdims=True)
    return centred * lax.rsqrt(variance + eps_norm) * gain_row + bias_row


def head_piece(pre_values, gain_row, bias_row, live_mask):
    return jax.nn.silu(layer_norm(pre_values, gain_row, bias_row)) * live_mask


def tail_piece(source, third_pre, gain_row, bias_row, live_mask):
    return jax.nn.silu(source + layer_norm(third_pre, gain_row, bias_row)) * live_mask


def outer_sum(left_rows, right_rows):
    return lax.dot_general(
        left_rows, right_rows, (((0,), (0,)), ((), ())), preferred_element_type=jnp.float32
    )


def times_transposed(left_rows, weight):
    return lax.dot_general(
        left_rows, weight, (((1,), (1,)), ((), ())), preferred_element_type=jnp.float32
    )


def pad_columns(values):
    return jnp.pad(values, ((0, 0), (0, 0), (1, 1), (0, 0)))


def rows_forward(hidden_one):
    return extended(hidden_one, (("row", 1),), 1)


def rows_backward(second_low):
    return extended(second_low, (("row", 1),), 1)


def depth_apply(padded, tap_table, row_count, col_count):
    result = jnp.zeros((padded.shape[0], row_count, col_count, padded.shape[3]), jnp.float32)
    for offset in range(9):
        window = padded[
            :, offset // 3 : offset // 3 + row_count, offset % 3 : offset % 3 + col_count, :
        ]
        result = result + window.astype(jnp.float32) * tap_table[offset].astype(jnp.float32)
    return result


def block_forward(source, live_mask, weights):
    w_first, w_last, tap_table, gain_rows, bias_rows = weights
    grid_count, row_count, col_count, channels = source.shape
    flat_rows = source.astype(jnp.bfloat16).reshape(-1, channels)
    first_pre = jnp.dot(flat_rows, w_first, preferred_element_type=jnp.float32).reshape(
        source.shape
    )
    hidden_one = head_piece(first_pre, gain_rows[0], bias_rows[0], live_mask).astype(jnp.bfloat16)
    padded_one = pad_columns(rows_forward(hidden_one))
    second_pre = depth_apply(padded_one, tap_table, row_count, col_count)
    hidden_two = head_piece(second_pre, gain_rows[1], bias_rows[1], live_mask).astype(jnp.bfloat16)
    two_rows = hidden_two.reshape(-1, channels)
    third_pre = jnp.dot(two_rows, w_last, preferred_element_type=jnp.float32).reshape(source.shape)
    output = tail_piece(source, third_pre, gain_rows[2], bias_rows[2], live_mask)
    return (output, (flat_rows, first_pre, padded_one, second_pre, two_rows, third_pre))


def block_backward(output_grad, source, live_mask, weights, kept):
    w_first, w_last, tap_table, gain_rows, bias_rows = weights
    flat_rows, first_pre, padded_one, second_pre, two_rows, third_pre = kept
    grid_count, row_count, col_count, channels = source.shape
    _, tail_back = jax.vjp(
        partial(tail_piece, live_mask=live_mask), source, third_pre, gain_rows[2], bias_rows[2]
    )
    residual_grad, third_grad, gain_three, bias_three = tail_back(output_grad)
    third_low = third_grad.astype(jnp.bfloat16).reshape(-1, channels)
    grad_last = outer_sum(two_rows, third_low)
    two_grad = times_transposed(third_low, w_last).reshape(source.shape)
    _, middle_back = jax.vjp(
        partial(head_piece, live_mask=live_mask), second_pre, gain_rows[1], bias_rows[1]
    )
    second_grad, gain_two, bias_two = middle_back(two_grad)
    second_low = second_grad.astype(jnp.bfloat16)
    padded_grad = pad_columns(rows_backward(second_low))
    one_grad = depth_apply(padded_grad, tap_table[::-1], row_count, col_count)
    second_wide = second_low.astype(jnp.float32)
    tap_grads = []
    for offset in range(9):
        window = padded_one[
            :, offset // 3 : offset // 3 + row_count, offset % 3 : offset % 3 + col_count, :
        ]
        tap_grads.append(jnp.sum(second_wide * window.astype(jnp.float32), axis=(0, 1, 2)))
    _, first_back = jax.vjp(
        partial(head_piece, live_mask=live_mask), first_pre, gain_rows[0], bias_rows[0]
    )
    first_grad, gain_one, bias_one = first_back(one_grad)
    first_low = first_grad.astype(jnp.bfloat16).reshape(-1, channels)
    grad_first = outer_sum(flat_rows, first_low)
    source_grad = residual_grad + times_transposed(first_low, w_first).reshape(source.shape)
    grads = (
        grad_first,
        grad_last,
        jnp.stack(tap_grads),
        jnp.stack([gain_one, gain_two, gain_three]),
        jnp.stack([bias_one, bias_two, bias_three]),
    )
    return (source_grad, grads)


def pool_weights(grid_side, row_shift, pooled_index, slot_index):
    place = slot_index - row_shift
    begin = pooled_index * grid_side // POOL
    finish = ((pooled_index + 1) * grid_side + POOL - 1) // POOL
    inside = (place >= begin) & (place < finish)
    return jnp.where(inside, 1.0, 0.0).astype(jnp.float32) / (finish - begin).astype(jnp.float32)


def on_device(
    patches,
    grid_sizes,
    conv_in,
    conv_out,
    depth_taps,
    norm_gain,
    norm_bias,
    read_in,
    read_bias,
    read_out,
    cotangent,
):
    grid_count, local_rows, grid_width, channels = patches.shape
    row_place = lax.axis_index("row")
    slot_rows = row_place * local_rows + jnp.arange(local_rows, dtype=jnp.int32)
    column_index = jnp.arange(grid_width, dtype=jnp.int32)
    row_shift = (grid_width - grid_sizes) // 2
    row_live = (slot_rows[None, :] >= row_shift[:, None]) & (
        slot_rows[None, :] < (row_shift + grid_sizes)[:, None]
    )
    col_live = column_index[None, :] < grid_sizes[:, None]
    live_mask = (row_live[:, :, None] & col_live[:, None, :]).astype(jnp.float32)[..., None]
    weights_one = (conv_in[0], conv_out[0], depth_taps[0], norm_gain[0], norm_bias[0])
    weights_two = (conv_in[1], conv_out[1], depth_taps[1], norm_gain[1], norm_bias[1])
    source = patches.astype(jnp.float32) * live_mask
    encoded, kept_one = block_forward(source, live_mask, weights_one)
    pool_local = POOL // lax.axis_size("row")
    pooled_index = row_place * pool_local + jnp.arange(pool_local, dtype=jnp.int32)
    side_shaped = grid_sizes[:, None, None]
    row_pool = pool_weights(
        side_shaped, row_shift[:, None, None], pooled_index[None, :, None], slot_rows[None, None, :]
    )
    col_pool = pool_weights(
        side_shaped,
        0,
        jnp.arange(POOL, dtype=jnp.int32)[None, :, None],
        column_index[None, None, :],
    )
    pooled = jnp.einsum("gir,gjw,grwc->gijc", row_pool, col_pool, encoded, precision=exact_mode)
    all_live = jnp.ones((grid_count, pool_local, POOL, 1), jnp.float32)
    abstract, kept_two = block_forward(pooled, all_live, weights_two)
    token_rows = abstract.astype(jnp.bfloat16).reshape(-1, channels)
    gathered = lax.all_gather(token_rows, "wide", axis=0, tiled=True)
    gelu_exact = partial(jax.nn.gelu, approximate=False)
    mixed_pre = jnp.dot(gathered, read_in, preferred_element_type=jnp.float32) + read_bias[0]
    hidden_wide, gelu_back = jax.vjp(gelu_exact, mixed_pre)
    hidden = hidden_wide.astype(jnp.bfloat16)
    partial_out = jnp.dot(hidden, read_out, preferred_element_type=jnp.float32)
    summed = (
        lax.psum_scatter(
            partial_out.astype(jnp.bfloat16), "wide", scatter_dimension=1, tiled=True
        ).astype(jnp.float32)
        + read_bias[1]
    )
    tokens = summed.astype(jnp.bfloat16).reshape(cotangent.shape)
    cot_local = cotangent.reshape(-1, cotangent.shape[-1])
    cot_all = lax.all_gather(cot_local, "wide", axis=1, tiled=True)
    hidden_grad = times_transposed(cot_all, read_out)
    mixed_grad = gelu_back(hidden_grad)[0].astype(jnp.bfloat16)
    grad_exit = outer_sum(hidden, cot_all)
    grad_entry = outer_sum(gathered, mixed_grad)
    bias_pair = jnp.stack(
        [
            jnp.sum(mixed_grad.astype(jnp.float32), axis=0),
            jnp.sum(cot_local.astype(jnp.float32), axis=0),
        ]
    )
    abstract_grad = lax.psum_scatter(
        times_transposed(mixed_grad, read_in).astype(jnp.bfloat16),
        "wide",
        scatter_dimension=0,
        tiled=True,
    ).astype(jnp.float32)
    grad_entry, bias_pair, grad_exit = (
        lax.psum(grad_entry.astype(jnp.bfloat16), ("dp", "row")).astype(jnp.float32),
        lax.psum(bias_pair.astype(jnp.bfloat16), ("dp", "row")).astype(jnp.float32),
        lax.psum(grad_exit.astype(jnp.bfloat16), ("dp", "row")).astype(jnp.float32),
    )
    pooled_grad, grads_two = block_backward(
        abstract_grad.reshape(abstract.shape), pooled, all_live, weights_two, kept_two
    )
    encoded_grad = jnp.einsum(
        "gir,gjw,gijc->grwc", row_pool, col_pool, pooled_grad, precision=exact_mode
    )
    source_grad, grads_one = block_backward(encoded_grad, source, live_mask, weights_one, kept_one)
    patch_grad = (source_grad * live_mask).astype(jnp.bfloat16)
    stacked = tuple((jnp.stack([grads_one[index], grads_two[index]]) for index in range(5)))
    totals = (
        lax.psum_scatter(stacked[0], ("dp", "wide"), scatter_dimension=2, tiled=True),
        lax.psum_scatter(stacked[1], ("dp", "wide"), scatter_dimension=2, tiled=True),
        lax.psum_scatter(stacked[2], ("dp", "wide"), scatter_dimension=2, tiled=True),
        lax.psum_scatter(stacked[3], ("dp", "wide"), scatter_dimension=2, tiled=True),
        lax.psum_scatter(stacked[4], ("dp", "wide"), scatter_dimension=2, tiled=True),
    )
    totals = (
        lax.psum(totals[0].astype(jnp.bfloat16), "row").astype(jnp.float32),
        lax.psum(totals[1].astype(jnp.bfloat16), "row").astype(jnp.float32),
        lax.psum(totals[2].astype(jnp.bfloat16), "row").astype(jnp.float32),
        lax.psum(totals[3].astype(jnp.bfloat16), "row").astype(jnp.float32),
        lax.psum(totals[4].astype(jnp.bfloat16), "row").astype(jnp.float32),
    )
    return (
        tokens,
        patch_grad,
        totals[0],
        totals[1],
        totals[2],
        totals[3],
        totals[4],
        grad_entry,
        bias_pair,
        grad_exit,
    )


def solution(mesh):
    placed = (
        P(("dp", "wide"), "row", None, None),
        P(("dp", "wide")),
        P(),
        P(),
        P(),
        P(),
        P(),
        P(None, "wide"),
        P(None, "wide"),
        P("wide", None),
        P("dp", "row", None, "wide"),
    )
    return jax.shard_map(
        on_device,
        mesh=mesh,
        in_specs=placed,
        out_specs=(
            P("dp", "row", None, "wide"),
            P(("dp", "wide"), "row", None, None),
            P(None, None, ("dp", "wide")),
            P(None, None, ("dp", "wide")),
            P(None, None, ("dp", "wide")),
            P(None, None, ("dp", "wide")),
            P(None, None, ("dp", "wide")),
            P(None, "wide"),
            P(None, "wide"),
            P("wide", None),
        ),
        check_vma=False,
    )
```

profile of v0, /device:TPU:17, one launch (start us, length us, event | category | flops | bytes accessed | tf_op | source)
XLA Modules:
  0.0 1481.4 jit_solution(2084787019406870212)
XLA Ops:
  11.8 5.2 fusion.180
  32.6 5.2 fusion.170
  52.3 9.7 fusion.1
  96.2 42.6 %all-gather.3.cloned.1.call-done = bf16[1152,1024]{1,0:T(8,128)(2,1)} async-done(((bf16[288,1024]{1,0:T(8,128)(2,1)}), bf16[1152,1024]{1,0:T(8,128)(2,1)}) %all-gather.3.cloned.1.call-update) | async-done | bytes 2359312 | tf_op jit(solution)/shard_map/all_gather | solution.py:191
  138.8 6.3 convolution_add_fusion
  145.1 160.8 %all-gather.5.cloned.1.call-done = bf16[1152,4096]{1,0:T(8,128)(2,1)} async-done(((bf16[1152,1024]{1,0:T(8,128)(2,1)}), bf16[1152,4096]{1,0:T(8,128)(2,1)}) %all-gather.5.cloned.1.call-update) | async-done | bytes 9437200 | tf_op jit(solution)/shard_map/all_gather | solution.py:205
  305.9 27.2 %fusion.158 = (bf16[1024]{0:T(1024)(128)(2,1)}, bf16[1152,1024]{1,0:T(8,128)(2,1)S(1)}, f32[1152,1024]{1,0:T(8,128)}) fusion(f32[1152,1024]{1,0:T(8,128)} %convolution_add_fusion, bf16[1152,4096]{1,0:T(8,128)(2,1)} %all-gather.5.cloned.1.call-done, bf16[1024,4096]{1,0:T(8,128)(2,1)} %param.20), kind=kOutput, calls=%fused_computation.375 | convolution fusion | flops 9749789696 | bytes 29624320 | tf_op jit(solution)/shard_map/dot_general | solution.py:54
  340.5 6.5 multiply_convert_fusion.1
  347.1 39.2 %reduce-scatter.14.cloned.1.call-done = bf16[288,1024]{1,0:T(8,128)(2,1)} async-done(((bf16[1152,1024]{1,0:T(8,128)(2,1)}), bf16[288,1024]{1,0:T(8,128)(2,1)}) %reduce-scatter.14.cloned.1.call-update) | async-done | bytes 589840 | tf_op jit(solution)/shard_map/reduce_scatter | solution.py:216
  406.6 13.2 convolution_convert_fusion.1
  430.3 8.4 fusion.40
  438.8 6.4 multiply_reduce_fusion
  458.6 8.8 fusion.32
  479.9 13.2 multiply_reduce_fusion.2
  497.3 6.6 convolution_convert_fusion.3
  520.2 13.6 copy.39
  548.2 13.4 copy.38
  561.6 698.3 %all-reduce.17 = (bf16[2,1024,1024]{1,0,2:T(2,128)(2,1)}, bf16[2,1024,1024]{1,0,2:T(2,128)(2,1)}) all-reduce(f32[2,1024,1024]{1,0,2:T(2,128)} %copy.38, f32[2,1024,1024]{1,0,2:T(2,128)} %copy.39), channel_id=4, replica_groups=mesh['dp'=4,'wide'=4,'row'=2] {'dp','wide'}, use_global_device_ids=true, to_apply=%region_26.27.clone | all-reduce | flops 4194304 | bytes 25165824
  1263.7 15.2 %convolution_convert_fusion = bf16[1152,4096]{1,0:T(8,128)(2,1)} fusion(bf16[1152,1024]{1,0:T(8,128)(2,1)} %multiply_convert_fusion.1, bf16[1024,4096]{1,0:T(8,128)(2,1)} %param.20), kind=kOutput, calls=%fused_computation.10 | convolution fusion | flops 9668395008 | bytes 20185088 | tf_op jit(solution)/shard_map/dot_general | solution.py:196
  1281.0 14.9 %psum.62 = bf16[2,1024]{1,0:T(2,128)(2,1)S(1)} all-reduce(bf16[2,1024]{1,0:T(2,128)(2,1)S(1)} %pad_maximum_fusion.13), channel_id=1, replica_groups=mesh['dp'=4,'wide'=4,'row'=2] {'dp','row'}, use_global_device_ids=true, to_apply=%region_69.70 | all-reduce | flops 2048 | bytes 8192 | tf_op jit(solution)/shard_map/psum | solution.py:224
  1297.5 8.6 multiply_convert_fusion
  1308.0 5.8 all-reduce.8
  1319.6 11.9 convert_element_type.602
  1335.1 125.8 %reduce-scatter.12.cloned.1.call-done = bf16[1152,1024]{1,0:T(8,128)(2,1)} async-done(((bf16[1152,4096]{1,0:T(8,128)(2,1)}), bf16[1152,1024]{1,0:T(8,128)(2,1)}) %reduce-scatter.12.cloned.1.call-update) | async-done | bytes 2359312 | tf_op jit(solution)/shard_map/reduce_scatter | solution.py:198
  (515 shorter events, 196.6 us)
Async XLA Ops:
  7.2 131.6 %copy-start = (bf16[1024,1024]{1,0:T(8,128)(2,1)S(1)}, bf16[1024,1024]{1,0:T(8,128)(2,1)}, u32[]{:S(2)}) copy-start(bf16[1024,1024]{1,0:T(8,128)(2,1)} %param.18) | copy-start | bytes 6291460
  7.2 131.6 %all-gather.3.cloned.1.call-start = ((), (), s32[]{:S(2)}) async-start(), calls=%async_computation.5 | async-start | bytes 2949120 | tf_op jit(solution)/shard_map/all_gather | solution.py:191
  10.2 57.2 %copy-start.115 = (f32[1,1,1024]{2,0,1:T(1,128)}, f32[1,1,1024]{2,0,1:T(1,128)S(1)}, u32[]{:S(2)}) copy-start(f32[1,1,1024]{2,0,1:T(1,128)S(1)} %get-tuple-element.149) | copy-start | bytes 12292
  11.6 55.7 %copy-start.82 = (f32[1,1,1024]{2,0,1:T(1,128)}, f32[1,1,1024]{2,0,1:T(1,128)S(1)}, u32[]{:S(2)}) copy-start(f32[1,1,1024]{2,0,1:T(1,128)S(1)} %get-tuple-element.143) | copy-start | bytes 12292
  21.1 7.7 collective-permute-start.1
  22.4 7.2 collective-permute-start
  68.0 5.8 collective-permute-start.3
  69.3 6.0 collective-permute-start.2
  85.1 220.8 %all-gather.5.cloned.1.call-start = ((), (), s32[]{:S(2)}) async-start(), calls=%async_computation.7 | async-start | bytes 11796480 | tf_op jit(solution)/shard_map/all_gather | solution.py:205
  94.8 291.5 %reduce-scatter.14.cloned.1.call-start = ((), (), s32[]{:S(2)}) async-start(), calls=%async_computation.8 | async-start | bytes 2949120 | tf_op jit(solution)/shard_map/reduce_scatter | solution.py:216
  338.5 958.0 %reduce-scatter.16.cloned.1.call-start = ((), (), s32[]{:S(2)}) async-start(), calls=%async_computation.9 | async-start | bytes 557056
  340.5 48.2 %copy-start.13 = (f32[4,1024,6,12]{1,3,2,0:T(8,128)S(1)}, f32[4,1024,6,12]{1,3,2,0:T(8,128)}, u32[]{:S(2)}) copy-start(f32[4,1024,6,12]{1,3,2,0:T(8,128)} %copy-done.12) | copy-start | bytes 3538948
  340.5 48.2 %copy-start.48 = (f32[4,6,12]{2,1,0:T(8,128)S(1)}, f32[4,6,12]{2,1,0:T(8,128)}, u32[]{:S(2)}) copy-start(f32[4,6,12]{2,1,0:T(8,128)} %copy-done.47) | copy-start | bytes 3460
  340.5 48.2 %copy-start.63 = (f32[4,6,12]{2,1,0:T(8,128)S(1)}, f32[4,6,12]{2,1,0:T(8,128)}, u32[]{:S(2)}) copy-start(f32[4,6,12]{2,1,0:T(8,128)} %copy-done.62) | copy-start | bytes 3460
  401.0 18.9 %collective-permute-start.5 = (bf16[4,1,12,1024]{3,2,1,0:T(8,128)(2,1)S(1)}, bf16[4,1,12,1024]{3,2,1,0:T(8,128)(2,1)S(1)}, u32[]{:S(2)}, u32[]{:S(2)}) collective-permute-start(bf16[4,1,12,1024]{3,2,1,0:T(8,128)(2,1)S(1)} %get-tuple-element.121), channel_id=1, source_target_pairs={{1,0},{3,2},{5,4},{7,6},{9,8},{11,10},{13,12},{15,14},{17,16},{19,... | collective-permute-start | bytes 294920 | tf_op jit(solution)/shard_map/ppermute | solution.py:25
  402.4 17.4 %collective-permute-start.4 = (bf16[4,1,12,1024]{3,2,1,0:T(8,128)(2,1)S(1)}, bf16[4,1,12,1024]{3,2,1,0:T(8,128)(2,1)S(1)}, u32[]{:S(2)}, u32[]{:S(2)}) collective-permute-start(bf16[4,1,12,1024]{3,2,1,0:T(8,128)(2,1)S(1)} %get-tuple-element.120), channel_id=1, source_target_pairs={{0,1},{2,3},{4,5},{6,7},{8,9},{10,11},{12,13},{14,15},{16,17},{18,... | collective-permute-start | bytes 294920 | tf_op jit(solution)/shard_map/ppermute | solution.py:23
  468.9 7.7 collective-permute-start.7
  470.2 6.6 collective-permute-start.6
  476.4 829.7 %reduce-scatter.18.cloned.1.call-start = ((), (), s32[]{:S(2)}) async-start(), calls=%async_computation.10 | async-start | bytes 557056
  495.1 811.9 %reduce-scatter.20.cloned.1.call-start = ((), (), s32[]{:S(2)}) async-start(), calls=%async_computation.11 | async-start | bytes 557056
  497.3 818.2 %all-reduce.14.cloned.1.call-start = ((), (), s32[]{:S(2)}) async-start(), calls=%async_computation.12 | async-start | bytes 20971520 | tf_op jit(solution)/shard_map/psum | solution.py:223
  504.0 827.5 %all-reduce.16.cloned.1.call-start = ((), (), s32[]{:S(2)}) async-start(), calls=%async_computation.13 | async-start | bytes 1048576 | tf_op jit(solution)/shard_map/psum | solution.py:244
  1263.6 197.3 %reduce-scatter.12.cloned.1.call-start = ((), (), s32[]{:S(2)}) async-start(), calls=%async_computation.6 | async-start | bytes 11796480 | tf_op jit(solution)/shard_map/reduce_scatter | solution.py:198
  1319.6 141.4 %copy-start.150 = (f32[1,1024]{1,0:T(1,128)S(1)}, f32[1,1024]{1,0:T(1,128)}, u32[]{:S(2)}) copy-start(f32[1,1024]{1,0:T(1,128)} %get-tuple-element.154) | copy-start | bytes 12292
  (167 other events, 1517.3 us)
Sparse Core Ops, SparseCore 0:
  85.2 53.4 all-gather.2
  140.9 164.9 all-gather.4
  338.7 47.5 reduce-scatter.13
  476.5 53.0 reduce-scatter.15
  534.0 56.4 reduce-scatter.17
  593.9 57.1 reduce-scatter.19
  655.4 173.8 all-reduce.13
  1263.7 32.3 all-reduce.15
  1298.6 162.2 reduce-scatter.11
where the time goes:
time: 1490 us; the launch traced here: 1480 us
  blocking collectives  719 us (48%)
  waiting for transfers between devices  372 us (25%)
  matrix products  139 us (9%)
  other arithmetic  115 us (8%)
  local copies, waits for them, and re-layouts  95.2 us (6%)
  starting transfers between devices  22.5 us (2%)
  between operations  17.8 us (1%)
    unnamed x1, blocking collectives  698 us
    all_gather x1, waiting for transfers between devices, on_device(): cot_all = lax.all_gather(cot_local, 'wide', axis=1, tiled=True)  161 us
    reduce_scatter x1, waiting for transfers between devices, on_device(): lax.psum_scatter(partial_out.astype(jnp.bfloat16), 'wide', scatter_dimens...  126 us
    dot_general x6, matrix products, times_transposed(): lax.dot_general(left_rows, weight, (((1,), (1,)), ((), ())), preferred_el...  48.1 us
    unnamed x368, local copies, waits for them, and re-layouts  45.8 us
    all_gather x1, waiting for transfers between devices, on_device(): gathered = lax.all_gather(token_rows, 'wide', axis=0, tiled=True)  42.6 us
    reduce_scatter x1, waiting for transfers between devices, on_device(): lax.psum_scatter(times_transposed(mixed_grad, read_in).astype(jnp.bfloat1...  39.2 us
    dot_general x6, matrix products, outer_sum(): lax.dot_general(left_rows, right_rows, (((0,), (0,)), ((), ())), preferre...  34.3 us
  transfers between devices with their start and end apart: 17, of which 9 were waited for; matrix products, arithmetic and copies ran while one was open for 12% of the time, Pallas kernels for 0%

commit v1 on v0

--- a/solution.py
+++ b/solution.py
@@ -1,9 +1,562 @@
-from functools import partial
+import functools
 
 import jax
 import jax.numpy as jnp
 from jax import lax
+from jax.experimental import pallas as pl
+from jax.experimental.pallas import tpu as pltpu
 from jax.sharding import PartitionSpec as P
+
+MESH = pl.DeviceIdType.MESH
+BF = jnp.bfloat16
+F32 = jnp.float32
+VMEM = pltpu.VMEM
+
+
+class Place:
+    def __init__(self, nz, ndp, nrow):
+        self.nz, self.ndp, self.nrow = nz, ndp, nrow
+        self.nx = ndp // 2
+        self.nq = self.nx * nrow
+        self.k = lax.axis_index("wide")
+        self.r = lax.axis_index("row")
+        d = lax.axis_index("dp")
+        self.c = lax.rem(d, 2)
+        self.x = d // 2
+        self.q = self.x * nrow + self.r
+
+    def at(self, q=None, c=None, k=None):
+        q = self.q if q is None else q
+        c = self.c if c is None else c
+        k = self.k if k is None else k
+        return {"dp": (q // self.nrow) * 2 + c, "row": lax.rem(q, self.nrow), "wide": k}
+
+    def chip(self, t):
+        return lax.rem(self.q + t, self.nq)
+
+    def deep(self, t):
+        return lax.rem(self.k + t, self.nz)
+
+    def peers(self):
+        return (
+            [self.at(q=self.chip(t)) for t in range(1, self.nq)]
+            + [self.at(c=1 - self.c)]
+            + [self.at(k=self.deep(t)) for t in range(1, self.nz)]
+        )
+
+    def greet(self):
+        barrier = pltpu.get_barrier_semaphore()
+        peers = self.peers()
+        for peer in peers:
+            pl.semaphore_signal(barrier, inc=1, device_id=peer, device_id_type=MESH)
+        pl.semaphore_wait(barrier, len(peers))
+
+
+class Links:
+    def __init__(self, send, recv):
+        self.send, self.recv, self.used = send, recv, 0
+
+    def copy(self, src, dst, peer):
+        at = self.used
+        self.used += 1
+        return pltpu.make_async_remote_copy(
+            src_ref=src, dst_ref=dst, send_sem=self.send.at[at], recv_sem=self.recv.at[at],
+            device_id=peer, device_id_type=MESH,
+        )
+
+
+def start_all(copies):
+    for copy in copies:
+        copy.start()
+    return copies
+
+
+def recv_all(copies):
+    for copy in copies:
+        copy.wait_recv()
+
+
+def sent_all(copies):
+    for copy in copies:
+        copy.wait_send()
+
+
+def rows_of(start, size, unit):
+    return pl.ds(pl.multiple_of(start, unit), size)
+
+
+def fold(out, parts, rows, step):
+    def body(i, carry):
+        at = rows_of(i * step, step, step)
+        total = parts[0](at).astype(F32)
+        for part in parts[1:]:
+            total = total + part(at).astype(F32)
+        out(at, total)
+        return carry
+
+    lax.fori_loop(0, rows // step, body, 0)
+
+
+def nt(a, b):
+    return lax.dot_general(a, b, (((1,), (1,)), ((), ())), preferred_element_type=F32)
+
+
+def nn(a, b):
+    return jnp.dot(a, b, preferred_element_type=F32)
+
+
+def tn(a, b):
+    return lax.dot_general(a, b, (((0,), (0,)), ((), ())), preferred_element_type=F32)
+
+
+def gelu_pair(v):
+    dense = jnp.exp(-0.5 * v * v)
+    s = 1.0 / (1.0 + (0.3275911 * 0.7071067811865476) * jnp.abs(v))
+    poly = s * (0.254829592 + s * (-0.284496736 + s * (1.421413741 + s * (-1.453152027 + s * 1.061405429))))
+    tail = 0.5 * poly * dense
+    phi = jnp.where(v >= 0, 1.0 - tail, tail)
+    return v * phi, phi + v * dense * 0.3989422804014327
+
+
+def readout_kernel(
+    nz, ndp, nrow,
+    mine, cot, rin_part, rout_part, bias_part, bias_out,
+    tokens, agrad, s1, f2, hsum, rc2, rp2,
+    rin, rout, bias, abst, abst_t, hid, mg, ag_send, ag_recv, s2, send, recv, local,
+):
+    me = Place(nz, ndp, nrow)
+    links = Links(send, recv)
+    T, C = mine.shape
+    hw, ow = rout.shape[1], rout.shape[2]
+    tall = nz * T
+    np_ = 2 * me.nq
+    strip = me.c * me.nq + me.q
+    ra, rb = C // np_, hw // np_
+    me.greet()
+
+    own = [
+        pltpu.make_async_copy(rin_part, rin.at[0], local.at[0]),
+        pltpu.make_async_copy(rout_part.at[:, rows_of(me.k * ow, ow, 128)], rout.at[0], local.at[1]),
+        pltpu.make_async_copy(mine, abst.at[rows_of(me.k * T, T, 16)], local.at[2]),
+    ]
+    for copy in own:
+        copy.start()
+    za, zb, zc = [], [], []
+    row_a = rows_of(strip * ra, ra, ra)
+    row_b = rows_of(strip * rb, rb, rb)
+    for t in range(1, nz):
+        there = lax.rem(me.k + nz - t, nz)
+        za.append(links.copy(rin_part.at[row_a], rin.at[t, row_a], me.at(k=there)))
+        zc.append(links.copy(bias_part, bias.at[t], me.at(k=there)))
+    start_all(za)
+    start_all(zc)
+    here = rows_of(me.k * T, T, 16)
+    zg = [links.copy(mine, abst.at[here], me.at(k=lax.rem(me.k + nz - t, nz))) for t in range(1, nz)]
+    start_all(zg)
+    for t in range(1, nz):
+        there = lax.rem(me.k + nz - t, nz)
+        zb.append(links.copy(
+            rout_part.at[row_b, rows_of(there * ow, ow, 128)], rout.at[t, row_b], me.at(k=there)))
+    start_all(zb)
+    bias[0] = bias_part[...]
+
+    def across(weights, row, height, arrived):
+        recv_all(arrived)
+        part = weights.at[pl.ds(1, nz - 1), row]
+        return start_all([links.copy(part, part, me.at(q=me.chip(t))) for t in range(1, me.nq)])
+
+    def between_cores(weights, height, arrived):
+        recv_all(arrived)
+        half = rows_of(me.c * (me.nq * height), me.nq * height, height)
+        part = weights.at[pl.ds(1, nz - 1), half]
+        return start_all([links.copy(part, part, me.at(c=1 - me.c))])
+
+    pa = across(rin, row_a, ra, za)
+    pb = across(rout, row_b, rb, zb)
+    ca = between_cores(rin, ra, pa)
+    cb = between_cores(rout, rb, pb)
+    for copy in own:
+        copy.wait()
+    recv_all(zc)
+    recv_all(ca)
+    recv_all(cb)
+
+    hsum[...] = jnp.zeros_like(hsum)
+    ag = [None] + [
+        links.copy(ag_send.at[t - 1], ag_recv.at[t - 1], me.at(k=me.deep(t))) for t in range(1, nz)
+    ]
+    NT = min(512, hw)
+
+    def group(t):
+        z = me.deep(t)
+        rows = rows_of(z * T, T, 16)
+
+        def unit(i, carry):
+            u = i // (hw // NT)
+            cols = rows_of(lax.rem(i, hw // NT) * NT, NT, 128)
+            pre = nn(abst[rows], rin[u, :, cols]) + bias[u, 0:1, cols]
+            up = nt(cot[rows], rout[u, cols, :])
+            value, slope = gelu_pair(pre)
+            hid[u, rows, cols] = value.astype(BF)
+            grad = (up * slope).astype(BF)
+            mg[u, rows, cols] = grad
+            hsum[me.deep(u), 0:1, cols] += jnp.sum(grad.astype(F32), axis=0, keepdims=True)
+            return carry
+
+        lax.fori_loop(0, nz * (hw // NT), unit, 0)
+        CT = 256
+
+        def back(i, carry):
+            at = rows_of(i * CT, CT, CT)
+            total = nt(mg[0, rows, :], rin[0, at, :])
+            for u in range(1, nz):
+                total = total + nt(mg[u, rows, :], rin[u, at, :])
+            if t == 0:
+                agrad[:, at] = total
+            else:
+                ag_send[t - 1, :, at] = total.astype(BF)
+            return carry
+
+        lax.fori_loop(0, C // CT, back, 0)
+
+    for t in range(nz):
+        if t:
+            zg[t - 1].wait_recv()
+        group(t)
+        if t:
+            ag[t].start()
+
+    HT = 256
+
+    def g2(i, carry):
+        u = i // (hw // HT)
+        at = rows_of(lax.rem(i, hw // HT) * HT, HT, HT)
+        s2[me.deep(u), at, :] = tn(hid[u, :, at], cot[...]).astype(BF)
+        return carry
+
+    lax.fori_loop(0, nz * (hw // HT), g2, 0)
+    half = me.nq * rb
+    theirs = rows_of((1 - me.c) * half, half, half)
+    core2 = start_all([links.copy(s2.at[:, theirs], rc2, me.at(c=1 - me.c))])
+
+    def f2_body(i, carry):
+        at = rows_of(i * 256, 256, 256)
+        total = nn(hid[0], rout[0, :, at]) + bias_out[0:1, at]
+        for u in range(1, nz):
+            total = total + nn(hid[u], rout[u, :, at])
+        tokens[:, at] = total.astype(BF)
+        return carry
+
+    lax.fori_loop(0, ow // 256, f2_body, 0)
+    recv_all(core2)
+    sent_all(core2)
+    loads = [
+        pltpu.make_async_copy(rc2.at[j], hid.at[j, pl.ds(0, half)], local.at[j]) for j in range(nz)
+    ]
+    for copy in loads:
+        copy.start()
+    for j in range(nz):
+        loads[j].wait()
+        fold(
+            lambda at, v, j=j: s2.__setitem__((j, rows_of(me.c * half + at.start, at.size, 16)), v.astype(BF)),
+            [lambda at, j=j: s2[j, rows_of(me.c * half + at.start, at.size, 16)], lambda at, j=j: hid[j, at]],
+            half, 32,
+        )
+    sends2 = []
+    for t in range(1, me.nq):
+        q = me.chip(t)
+        src = s2.at[:, rows_of((me.c * me.nq + q) * rb, rb, rb)]
+        sends2.append(links.copy(src, rp2.at[t - 1], me.at(q=q)))
+    start_all(sends2)
+
+    abst_t[...] = abst[...].T
+
+    def g1(i, carry):
+        u = i // (C // 256)
+        at = rows_of(lax.rem(i, C // 256) * 256, 256, 256)
+        hid[u, at, :] = nn(abst_t[at, :], mg[u]).astype(BF)
+        return carry
+
+    lax.fori_loop(0, nz * (C // 256), g1, 0)
+    outs = [
+        pltpu.make_async_copy(hid.at[u, pl.ds(0, C)], s1.at[me.deep(u)], local.at[2 + u]) for u in range(nz)
+    ]
+    for copy in outs:
+        copy.start()
+    recv_all(ag[1:])
+    fold(
+        lambda at, v: agrad.__setitem__(at, v),
+        [lambda at: agrad[at]] + [lambda at, t=t: ag_recv[t - 1, at] for t in range(1, nz)],
+        T, 32,
+    )
+    for copy in outs:
+        copy.wait()
+    recv_all(sends2)
+    loads = [
+        pltpu.make_async_copy(rp2.at[t - 1], mg.at[pl.ds(0, nz), pl.ds(t * rb, rb)], local.at[t - 1])
+        for t in range(1, me.nq)
+    ]
+    for copy in loads:
+        copy.start()
+    for copy in loads:
+        copy.wait()
+    for j in range(nz):
+        fold(
+            lambda at, v, j=j: f2.__setitem__((j, at), v.astype(BF)),
+            [lambda at, j=j: s2[j, rows_of(strip * rb + at.start, at.size, 16)]]
+            + [lambda at, j=j, t=t: mg[j, rows_of(t * rb + at.start, at.size, 16)] for t in range(1, me.nq)],
+            rb, min(rb, 32),
+        )
+    for group_of in (za, zb, zc, zg, pa, pb, ca, cb, ag[1:], sends2):
+        sent_all(group_of)
+
+
+def grads_kernel(
+    nz, ndp, nrow,
+    s1, f2, conv, small,
+    out1, out2, out3, small_out,
+    m1, rc1, rp1, f1, rz1, m3, rc3, rp3, f3, rz3, sc, sp, sz, send, recv, local,
+):
+    me = Place(nz, ndp, nrow)
+    links = Links(send, recv)
+    C, hw = out1.shape
+    ow = f2.shape[2]
+    np_ = 2 * me.nq
+    strip = me.c * me.nq + me.q
+    ra, rb = C // np_, hw // np_
+    width = C // nrow
+    R = out3.shape[2] // 2
+    other = me.at(c=1 - me.c)
+    half = me.nq * ra
+    me.greet()
+
+    sums = start_all([links.copy(small, sc, other)])
+    theirs = rows_of((1 - me.c) * half, half, half)
+    core3 = [links.copy(conv.at[b, :, :, 1 - me.c], rc3.at[b], other) for b in range(2)]
+    core1 = links.copy(s1.at[:, theirs], rc1, other)
+    core1.start()
+    start_all(core3)
+    row_b = rows_of(strip * rb, rb, rb)
+    col_k = rows_of(me.k * ow, ow, 128)
+    z2 = start_all([
+        links.copy(f2.at[me.deep(t)], out2.at[row_b, col_k], me.at(k=me.deep(t))) for t in range(1, nz)
+    ])
+    own = [
+        pltpu.make_async_copy(s1.at[:, rows_of(me.c * half, half, half)], m1, local.at[0]),
+        pltpu.make_async_copy(conv.at[0, :, :, me.c], m3.at[0], local.at[1]),
+        pltpu.make_async_copy(conv.at[1, :, :, me.c], m3.at[1], local.at[2]),
+    ]
+    for copy in own:
+        copy.start()
+    out2[row_b, col_k] = f2[me.k]
+    recv_all(sums)
+    sent_all(sums)
+    small_out[...] = small[...] + sc[...]
+    sums_p = start_all([links.copy(small_out, sp.at[t - 1], me.at(q=me.chip(t))) for t in range(1, me.nq)])
+
+    for copy in own:
+        copy.wait()
+    core1.wait_recv()
+    for j in range(nz):
+        fold(
+            lambda at, v, j=j: m1.__setitem__((j, at), v.astype(BF)),
+            [lambda at, j=j: m1[j, at], lambda at, j=j: rc1[j, at]],
+            half, 32,
+        )
+    p1 = start_all([
+        links.copy(m1.at[:, rows_of(me.chip(t) * ra, ra, ra)], rp1.at[t - 1], me.at(q=me.chip(t)))
+        for t in range(1, me.nq)
+    ])
+    p3 = []
+    for b in range(2):
+        core3[b].wait_recv()
+        for m in range(2):
+            for x in range(me.nx):
+                fold(
+                    lambda at, v, i=(b, m, x): m3.__setitem__((*i, at), v.astype(BF)),
+                    [lambda at, i=(b, m, x): m3[(*i, at)], lambda at, i=(b, m, x): rc3[(*i, at)]],
+                    nz * R, 32,
+                )
+        sends = []
+        for t in range(1, me.nq):
+            q = me.chip(t)
+            cols = rows_of(lax.rem(q, nrow) * width, width, 128)
+            sends.append(links.copy(m3.at[b, :, q // nrow, :, cols], rp3.at[b, t - 1], me.at(q=q)))
+        p3.append(start_all(sends))
+
+    recv_all(z2)
+    g2 = start_all([
+        links.copy(out2.at[row_b], out2.at[row_b], me.at(q=me.chip(t))) for t in range(1, me.nq)
+    ])
+
+    sent_all(sums_p)
+    recv_all(sums_p)
+    for t in range(1, me.nq):
+        small_out[...] += sp[t - 1]
+    sums_z = start_all([links.copy(small_out, sz.at[t - 1], me.at(k=me.deep(t))) for t in range(1, nz)])
+
+    recv_all(p1)
+    mine = rows_of(me.q * ra, ra, ra)
+    for j in range(nz):
+        fold(
+            lambda at, v, j=j: f1.__setitem__((j, at), v.astype(BF)),
+            [lambda at, j=j: m1[j, rows_of(me.q * ra + at.start, at.size, 16)]]
+            + [lambda at, j=j, t=t: rp1[t - 1, j, at] for t in range(1, me.nq)],
+            ra, 32,
+        )
+    z1 = start_all([links.copy(f1.at[me.deep(t)], rz1.at[t - 1], me.at(k=me.deep(t))) for t in range(1, nz)])
+    z3 = []
+    my_cols = rows_of(me.r * width, width, 128)
+    for b in range(2):
+        recv_all(p3[b])
+        for m in range(2):
+            for j in range(nz):
+                rows = pl.ds(j * R, R)
+                total = m3[b, m, me.x, rows, my_cols].astype(F32)
+                for t in range(1, me.nq):
+                    total = total + rp3[b, t - 1, m, rows, :].astype(F32)
+                f3[b, j, pl.ds(m * R, R)] = total.astype(BF)
+        z3.append(start_all([
+            links.copy(f3.at[b, me.deep(t)], rz3.at[b, t - 1], me.at(k=me.deep(t))) for t in range(1, nz)
+        ]))
+
+    recv_all(z1)
+    row_a = rows_of(strip * ra, ra, ra)
+    fold(
+        lambda at, v: out1.__setitem__(rows_of(strip * ra + at.start, at.size, 16), v.astype(BF)),
+        [lambda at: f1[me.k, at]] + [lambda at, t=t: rz1[t - 1, at] for t in range(1, nz)],
+        ra, 32,
+    )
+    g1 = start_all([
+        links.copy(out1.at[row_a], out1.at[row_a], me.at(q=me.chip(t))) for t in range(1, me.nq)
+    ])
+    g3 = []
+    for b in range(2):
+        recv_all(z3[b])
+        total = f3[b, me.k].astype(F32)
+        for t in range(1, nz):
+            total = total + rz3[b, t - 1].astype(F32)
+        out3[b, me.r] = total.astype(BF)
+        g3 += start_all([
+            links.copy(out3.at[b, me.r], out3.at[b, me.r], me.at(q=me.x * nrow + lax.rem(me.r + t, nrow)))
+            for t in range(1, nrow)
+        ])
+    recv_all(g2)
+    half_b = rows_of(me.c * me.nq * rb, me.nq * rb, me.nq * rb)
+    h2 = start_all([links.copy(out2.at[half_b], out2.at[half_b], other)])
+    recv_all(g1)
+    half_a = rows_of(me.c * half, half, half)
+    h1 = start_all([links.copy(out1.at[half_a], out1.at[half_a], other)])
+    sent_all(sums_z)
+    recv_all(sums_z)
+    for t in range(1, nz):
+        small_out[...] += sz[t - 1]
+    recv_all(g3)
+    recv_all(h1)
+    recv_all(h2)
+    for group_of in ([core1], core3, z2, p1, p3[0], p3[1], g2, z1, z3[0], z3[1], g1, g3, h1, h2):
+        sent_all(group_of)
+
+
+def spec(*kinds):
+    return [pl.BlockSpec(memory_space=kind) for kind in kinds]
+
+
+def run_readout(mesh, token_rows, cot, read_in, read_out, read_bias):
+    nz, ndp, nrow = mesh.shape["wide"], mesh.shape["dp"], mesh.shape["row"]
+    nq = ndp // 2 * nrow
+    T, C = token_rows.shape
+    hw, ow = read_out.shape[0], cot.shape[1]
+    tall = nz * T
+    rb = hw // (2 * nq)
+    copies = 4 * (nz - 1) + 2 * (nq - 1) + 2 + (nz - 1) + 1 + (nq - 1)
+    bias_part = jnp.broadcast_to(read_bias[0:1], (8, hw))
+    bias_out = jnp.broadcast_to(read_bias[1:2], (8, ow))
+    ANY = pl.ANY
+    return pl.pallas_call(
+        functools.partial(readout_kernel, nz, ndp, nrow),
+        out_shape=[
+            jax.ShapeDtypeStruct((tall, ow), BF),
+            jax.ShapeDtypeStruct((T, C), F32),
+            jax.ShapeDtypeStruct((nz, C, hw), BF),
+            jax.ShapeDtypeStruct((nz, rb, ow), BF),
+            jax.ShapeDtypeStruct((nz, 1, hw), F32),
+            jax.ShapeDtypeStruct((nz, nq * rb, ow), BF),
+            jax.ShapeDtypeStruct((nq - 1, nz, rb, ow), BF),
+        ],
+        in_specs=spec(ANY, VMEM, ANY, ANY, VMEM, VMEM),
+        out_specs=spec(VMEM, VMEM, ANY, VMEM, VMEM, ANY, ANY),
+        scratch_shapes=[
+            VMEM((nz, C, hw), BF),
+            VMEM((nz, hw, ow), BF),
+            VMEM((nz, 8, hw), F32),
+            VMEM((tall, C), BF),
+            VMEM((C, tall), BF),
+            VMEM((nz, tall, hw), BF),
+            VMEM((nz, tall, hw), BF),
+            VMEM((nz - 1, T, C), BF),
+            VMEM((nz - 1, T, C), BF),
+            VMEM((nz, hw, ow), BF),
+            pltpu.SemaphoreType.DMA((copies,)),
+            pltpu.SemaphoreType.DMA((copies,)),
+            pltpu.SemaphoreType.DMA((nz + 2,)),
+        ],
+        compiler_params=pltpu.CompilerParams(
+            collective_id=0, has_side_effects=True, vmem_limit_bytes=LIMIT
+        ),
+        name="readout",
+    )(token_rows, cot, read_in, read_out, bias_part, bias_out)
+
+
+LIMIT = 60 * 1024 * 1024
+
+
+def run_grads(mesh, s1, f2, conv, small):
+    nz, ndp, nrow = mesh.shape["wide"], mesh.shape["dp"], mesh.shape["row"]
+    nq = ndp // 2 * nrow
+    nx = ndp // 2
+    _, C, hw = s1.shape
+    _, rb, ow = f2.shape
+    ra = C // (2 * nq)
+    R = C // (ndp * nz)
+    S = small.shape[0]
+    copies = 3 + 1 + (nz - 1) + (nq - 1) * 2 + 2 * (nq - 1) + (nq - 1) + (nz - 1) * 2 + 2 * (nz - 1) + (nq - 1) + 2 * (nrow - 1) + 2
+    width = C // nrow
+    ANY = pl.ANY
+    return pl.pallas_call(
+        functools.partial(grads_kernel, nz, ndp, nrow),
+        out_shape=[
+            jax.ShapeDtypeStruct((C, hw), BF),
+            jax.ShapeDtypeStruct((hw, nz * ow), BF),
+            jax.ShapeDtypeStruct((2, nrow, 2 * R, width), BF),
+            jax.ShapeDtypeStruct((S, C), F32),
+        ],
+        in_specs=spec(ANY, VMEM, ANY, VMEM),
+        out_specs=spec(VMEM, VMEM, VMEM, VMEM),
+        scratch_shapes=[
+            VMEM((nz, C // 2, hw), BF),
+            VMEM((nz, C // 2, hw), BF),
+            VMEM((nq - 1, nz, ra, hw), BF),
+            VMEM((nz, ra, hw), BF),
+            VMEM((nz - 1, ra, hw), BF),
+            VMEM((2, 2, nx, nz * R, C), BF),
+            VMEM((2, 2, nx, nz * R, C), BF),
+            VMEM((2, nq - 1, 2, nz * R, width), BF),
+            VMEM((2, nz, 2 * R, width), BF),
+            VMEM((2, nz - 1, 2 * R, width), BF),
+            VMEM((S, C), F32),
+            VMEM((nq - 1, S, C), F32),
+            VMEM((nz - 1, S, C), F32),
+            pltpu.SemaphoreType.DMA((copies,)),
+            pltpu.SemaphoreType.DMA((copies,)),
+            pltpu.SemaphoreType.DMA((3,)),
+        ],
+        compiler_params=pltpu.CompilerParams(
+            collective_id=1, has_side_effects=True, vmem_limit_bytes=LIMIT
+        ),
+        name="grads",
+    )(s1, f2, conv, small)
+
 
 POOL = 12
 
@@ -95,19 +648,19 @@
     return (output, (flat_rows, first_pre, padded_one, second_pre, two_rows, third_pre))
 
 
-def block_backward(output_grad, source, live_mask, weights, kept):
+def block_backward(output_grad, source, live_mask, weights, kept, turned=False):
     w_first, w_last, tap_table, gain_rows, bias_rows = weights
     flat_rows, first_pre, padded_one, second_pre, two_rows, third_pre = kept
     grid_count, row_count, col_count, channels = source.shape
     _, tail_back = jax.vjp(
-        partial(tail_piece, live_mask=live_mask), source, third_pre, gain_rows[2], bias_rows[2]
+        functools.partial(tail_piece, live_mask=live_mask), source, third_pre, gain_rows[2], bias_rows[2]
     )
     residual_grad, third_grad, gain_three, bias_three = tail_back(output_grad)
     third_low = third_grad.astype(jnp.bfloat16).reshape(-1, channels)
-    grad_last = outer_sum(two_rows, third_low)
+    grad_last = outer_sum(third_low, two_rows) if turned else outer_sum(two_rows, third_low)
     two_grad = times_transposed(third_low, w_last).reshape(source.shape)
     _, middle_back = jax.vjp(
-        partial(head_piece, live_mask=live_mask), second_pre, gain_rows[1], bias_rows[1]
+        functools.partial(head_piece, live_mask=live_mask), second_pre, gain_rows[1], bias_rows[1]
     )
     second_grad, gain_two, bias_two = middle_back(two_grad)
     second_low = second_grad.astype(jnp.bfloat16)
@@ -121,11 +674,11 @@
         ]
         tap_grads.append(jnp.sum(second_wide * window.astype(jnp.float32), axis=(0, 1, 2)))
     _, first_back = jax.vjp(
-        partial(head_piece, live_mask=live_mask), first_pre, gain_rows[0], bias_rows[0]
+        functools.partial(head_piece, live_mask=live_mask), first_pre, gain_rows[0], bias_rows[0]
     )
     first_grad, gain_one, bias_one = first_back(one_grad)
     first_low = first_grad.astype(jnp.bfloat16).reshape(-1, channels)
-    grad_first = outer_sum(flat_rows, first_low)
+    grad_first = outer_sum(first_low, flat_rows) if turned else outer_sum(flat_rows, first_low)
     source_grad = residual_grad + times_transposed(first_low, w_first).reshape(source.shape)
     grads = (
         grad_first,
@@ -145,7 +698,7 @@
     return jnp.where(inside, 1.0, 0.0).astype(jnp.float32) / (finish - begin).astype(jnp.float32)
 
 
-def on_device(
+def plain(
     patches,
     grid_sizes,
     conv_in,
@@ -189,7 +742,7 @@
     abstract, kept_two = block_forward(pooled, all_live, weights_two)
     token_rows = abstract.astype(jnp.bfloat16).reshape(-1, channels)
     gathered = lax.all_gather(token_rows, "wide", axis=0, tiled=True)
-    gelu_exact = partial(jax.nn.gelu, approximate=False)
+    gelu_exact = functools.partial(jax.nn.gelu, approximate=False)
     mixed_pre = jnp.dot(gathered, read_in, preferred_element_type=jnp.float32) + read_bias[0]
     hidden_wide, gelu_back = jax.vjp(gelu_exact, mixed_pre)
     hidden = hidden_wide.astype(jnp.bfloat16)
@@ -261,7 +814,109 @@
     )
 
 
+def on_device(
+    mesh,
+    patches,
+    grid_sizes,
+    conv_in,
+    conv_out,
+    depth_taps,
+    norm_gain,
+    norm_bias,
+    read_in,
+    read_bias,
+    read_out,
+    cotangent,
+):
+    nz, ndp = mesh.shape["wide"], mesh.shape["dp"]
+    grid_count, local_rows, grid_width, channels = patches.shape
+    row_place = lax.axis_index("row")
+    slot_rows = row_place * local_rows + jnp.arange(local_rows, dtype=jnp.int32)
+    column_index = jnp.arange(grid_width, dtype=jnp.int32)
+    row_shift = (grid_width - grid_sizes) // 2
+    row_live = (slot_rows[None, :] >= row_shift[:, None]) & (
+        slot_rows[None, :] < (row_shift + grid_sizes)[:, None]
+    )
+    col_live = column_index[None, :] < grid_sizes[:, None]
+    live_mask = (row_live[:, :, None] & col_live[:, None, :]).astype(jnp.float32)[..., None]
+    weights_one = (conv_in[0], conv_out[0], depth_taps[0], norm_gain[0], norm_bias[0])
+    weights_two = (conv_in[1], conv_out[1], depth_taps[1], norm_gain[1], norm_bias[1])
+    source = patches.astype(jnp.float32) * live_mask
+    encoded, kept_one = block_forward(source, live_mask, weights_one)
+    pool_local = POOL // lax.axis_size("row")
+    pooled_index = row_place * pool_local + jnp.arange(pool_local, dtype=jnp.int32)
+    side_shaped = grid_sizes[:, None, None]
+    row_pool = pool_weights(
+        side_shaped, row_shift[:, None, None], pooled_index[None, :, None], slot_rows[None, None, :]
+    )
+    col_pool = pool_weights(
+        side_shaped,
+        0,
+        jnp.arange(POOL, dtype=jnp.int32)[None, :, None],
+        column_index[None, None, :],
+    )
+    pooled = jnp.einsum("gir,gjw,grwc->gijc", row_pool, col_pool, encoded, precision=exact_mode)
+    all_live = jnp.ones((grid_count, pool_local, POOL, 1), jnp.float32)
+    abstract, kept_two = block_forward(pooled, all_live, weights_two)
+    token_rows = abstract.astype(jnp.bfloat16).reshape(-1, channels)
+    cot_local = cotangent.reshape(-1, cotangent.shape[-1])
+    tokens, abstract_grad, s1, f2, hsum, _, _ = run_readout(
+        mesh, token_rows, cot_local, read_in, read_out, read_bias
+    )
+    tokens = tokens.reshape(cotangent.shape)
+    pooled_grad, grads_two = block_backward(
+        abstract_grad.reshape(abstract.shape), pooled, all_live, weights_two, kept_two, True
+    )
+    encoded_grad = jnp.einsum(
+        "gir,gjw,gijc->grwc", row_pool, col_pool, pooled_grad, precision=exact_mode
+    )
+    source_grad, grads_one = block_backward(encoded_grad, source, live_mask, weights_one, kept_one, True)
+    patch_grad = (source_grad * live_mask).astype(jnp.bfloat16)
+    R = channels // (ndp * nz)
+    conv = jnp.stack(
+        [jnp.stack([g[0].astype(BF), g[1].astype(BF)]) for g in (grads_one, grads_two)]
+    ).reshape(2, 2, ndp // 2, 2, nz * R, channels)
+    cot_sum = jnp.sum(cot_local.astype(F32), axis=0)
+    width = cot_sum.shape[0]
+    cot_row = lax.dynamic_update_slice(
+        jnp.zeros((nz * width,), F32), cot_sum, (lax.axis_index("wide") * width,)
+    )
+    small = jnp.concatenate(
+        [piece for g in (grads_one, grads_two) for piece in g[2:]]
+        + [hsum.reshape(-1, channels), cot_row.reshape(-1, channels)]
+    )
+    lines = small.shape[0]
+    small = jnp.pad(small, ((0, -lines % 8), (0, 0)))
+    out1, out2, out3, small = run_grads(mesh, s1, f2, conv, small)
+    out3 = out3.reshape(2, -1, 2, R, out3.shape[-1]).transpose(0, 2, 1, 4, 3).reshape(2, 2, channels, R).astype(F32)
+    place = lax.axis_index("dp") * nz + lax.axis_index("wide")
+    own = lax.dynamic_slice_in_dim(small, place * R, R, axis=1)
+    taps = jnp.stack([own[0:9], own[15:24]])
+    gains = jnp.stack([own[9:12], own[24:27]])
+    biases = jnp.stack([own[12:15], own[27:30]])
+    per = (lines - 30) // 2
+    flat = small[30:lines].reshape(2, per * channels)
+    bias_pair = lax.dynamic_slice_in_dim(flat, lax.axis_index("wide") * width, width, axis=1)
+    return (
+        tokens,
+        patch_grad,
+        out3[:, 0],
+        out3[:, 1],
+        taps,
+        gains,
+        biases,
+        out1.astype(F32),
+        bias_pair,
+        out2.astype(F32),
+    )
+
+
+def fits(mesh):
+    return mesh.shape["wide"] <= 4 and mesh.shape["dp"] % 2 == 0
+
+
 def solution(mesh):
+
     placed = (
         P(("dp", "wide"), "row", None, None),
         P(("dp", "wide")),
@@ -276,7 +931,7 @@
         P("dp", "row", None, "wide"),
     )
     return jax.shard_map(
-        on_device,
+        functools.partial(on_device, mesh) if fits(mesh) else plain,
         mesh=mesh,
         in_specs=placed,
         out_specs=(

time: 1490 us -> 694 us (0.47)
  blocking collectives: 719 us -> 0 us
  Pallas kernels: 0 us -> 445 us
  waiting for transfers between devices: 372 us -> 5.17 us
  matrix products: 139 us -> 64.2 us
  local copies, waits for them, and re-layouts: 95.2 us -> 52.7 us
  other arithmetic: 115 us -> 97.1 us
    unnamed x1 -> x0, blocking collectives: 698 us -> none
    pallas_call x0 -> x2, Pallas kernels: none -> 445 us  [the longest x1 274 us: run_readout(): pl.pallas_call(functools.partial(readout_kernel, nz, ndp, nrow), out_shap...]
    all_gather x2 -> x0, waiting for transfers between devices: 203 us -> none  [the longest x1 161 us: on_device(): cot_all = lax.all_gather(cot_local, 'wide', axis=1, tiled=True)]
    reduce_scatter x2 -> x0, waiting for transfers between devices: 165 us -> none  [the longest x1 126 us: on_device(): lax.psum_scatter(partial_out.astype(jnp.bfloat16), 'wide', scatter_dimens...]
    dot_general x6 -> x4, matrix products: 48.1 us -> 14 us  [times_transposed(): lax.dot_general(left_rows, weight, (((1,), (1,)), ((), ())), preferred_el...]
    another operation x6 -> x2, local copies, waits for them, and re-layouts: 27.2 us -> 1.69 us  [the longest x1 0.85 us: on_device(): taps = jnp.stack([own[0:9], own[15:24]])]
    dot_general x2 -> x0, matrix products: 21.5 us -> none  [the longest x1 15.2 us: on_device(): partial_out = jnp.dot(hidden, read_out, preferred_element_type=jnp.float32)]
    psum x2 -> x0, blocking collectives: 20.7 us -> none  [the longest x1 14.9 us: on_device(): lax.psum(bias_pair.astype(jnp.bfloat16), ('dp', 'row')).astype(jnp.float32)]
  transfers between devices with their start and end apart: 17 -> 8, of which waited for: 9 -> 2; matrix products, arithmetic and copies ran while one was open for 12% -> 4% of each run, Pallas kernels for 0% -> 0%
where the time goes in v1:
time: 694 us; the launch traced here: 686 us
  Pallas kernels  445 us (64%)
  other arithmetic  97.1 us (14%)
  matrix products  64.2 us (9%)
  local copies, waits for them, and re-layouts  52.7 us (8%)
  starting transfers between devices  18.6 us (3%)
    pallas_call x1, Pallas kernels, run_readout(): pl.pallas_call(functools.partial(readout_kernel, nz, ndp, nrow), out_shap...  274 us
    pallas_call x1, Pallas kernels, run_grads(): pl.pallas_call(functools.partial(grads_kernel, nz, ndp, nrow), out_shape=...  171 us
    reduce_sum x6, other arithmetic, layer_norm(): return centred * lax.rsqrt(variance + eps_norm) * gain_row + bias_row  28.9 us
    unnamed x336, local copies, waits for them, and re-layouts  25.4 us
    dot_general x4, matrix products, outer_sum(): lax.dot_general(left_rows, right_rows, (((0,), (0,)), ((), ())), preferre...  15.5 us
    reduce_sum x2, other arithmetic, block_backward(): jnp.sum(second_wide * window.astype(jnp.float32), axis=(0, 1, 2))  14.1 us
    dot_general x4, matrix products, times_transposed(): lax.dot_general(left_rows, weight, (((1,), (1,)), ((), ())), preferred_el...  14 us
  transfers between devices with their start and end apart: 8, of which 2 were waited for; matrix products, arithmetic and copies ran while one was open for 4% of the time, Pallas kernels for 0%

profile of v1, /device:TPU:17, one launch (start us, length us, event | category | flops | bytes accessed | tf_op | source)
XLA Modules:
  0.0 686.3 jit_solution(9782213219543644086)
XLA Ops:
  2.2 5.2 fusion.172
  24.2 5.2 fusion.162
  33.4 4.3 fusion.173
  43.9 9.0 %fusion.1 = f32[4,24,1024,6]{2,3,1,0:T(8,128)S(1)} fusion(f32[4,12,24,1024]{3,2,1,0:T(8,128)S(1)} %multiply_multiply_fusion, f32[4,6]{1,0:T(4,128)S(1)} %get-tuple-element.163, s32[4,6]{1,0:T(4,128)S(1)} %get-tuple-element.164, s32[4,6]{1,0:T(4,128)S(1)} %get-tuple-element.162, s32[4,12]{1,0:T(4,128)S(1)} %broadcast_subtract_fusion), kind=kOutput, calls=%fused_computation.20 | convolution fusion | flops 84936096 | bytes 7078368 | tf_op jit(solution)/shard_map/gir,gjw,grwc->gijc/dot_general | solution.py:858
  66.0 4.9 reshape.949.cot
  87.6 274.1 %readout.1 = (bf16[1152,1024]{1,0:T(8,128)(2,1)}, f32[288,1024]{1,0:T(8,128)}, bf16[4,1024,1024]{2,1,0:T(8,128)(2,1)}, bf16[4,128,1024]{2,1,0:T(8,128)(2,1)}, f3...) custom-call(bf16[288,1024]{1,0:T(8,128)(2,1)} %reshape.948.mine, ...), custom_call_target="tpu_custom_call" | custom-call | tf_op jit(solution)/shard_map/readout/pallas_call | solution.py:476
  364.2 4.5 multiply_reduce_fusion.9
  374.4 5.3 fusion.93
  379.8 4.3 collective-permute-start.4
  389.0 5.2 reshape.950
  394.3 4.8 copy.31
  400.4 3.9 multiply_reduce_fusion.11
  410.5 8.4 %fusion.34 = f32[4,1024,24,12]{1,3,2,0:T(8,128)S(1)} fusion(f32[4,6,1024,24]{2,3,1,0:T(8,128)S(1)} %fusion.94, f32[4,6]{1,0:T(4,128)S(1)} %copy-done.66, s32[4,6]{1,0:T(4,128)S(1)} %copy-done.68, s32[4,6]{1,0:T(4,128)S(1)} %copy-done.64, s32[4,12]{1,0:T(4,128)S(1)} %copy-done.62), kind=kOutput, calls=%fused_computation.107 | convolution fusion | flops 84936096 | bytes 7078368 | tf_op jit(solution)/shard_map/gir,gjw,gijc->grwc/dot_general | solution.py:870
  418.9 6.3 multiply_reduce_fusion
  427.2 6.7 fusion.148
  433.8 5.4 bitcast_convert_fusion.2
  441.6 8.8 %fusion.31 = (f32[1024]{0:T(1024)S(1)}, f32[1024]{0:T(1024)S(1)}, f32[1024]{0:T(1024)S(1)}, f32[1024]{0:T(1024)S(1)}, f32[1024]{0:T(1024)S(1)}, /*index=5*/f32[1...) fusion(bf16[4,14,26,1024]{3,2,1,0:T(8,128)(2,1)S(1)} %copy-done.1, ...), kind=kLoop, calls=%fused_computation.69 | loop fusion | flops 44817408 | bytes 28764160 | tf_op jit(solution)/shard_map/reduce_sum | solution.py:675
  450.5 4.0 collective-permute-start.6
  463.3 10.4 %multiply_reduce_fusion.2 = (f32[1024]{0:T(1024)S(1)}, f32[4,12,24]{2,1,0:T(8,128)S(1)}, f32[1024]{0:T(1024)S(1)}, f32[4,12,24,1024]{3,2,1,0:T(8,128)S(1)}) fusion(f32[4,12,24,1024]{3,2,1,0:T(8,128)S(1)} %bitcast.209, f32[4,12,24]{2,1,0:T(8,128)S(1)} %copy-done.39, f32[4,12,24]{2,1,0:T(8,128)S(1)} %copy-done.35, f32[1024]{0:T(1024)S(1)} %bitcast.225, ...), kind=kLoop, calls=%fused_computation.74 | loop fusion | flops 56619904 | bytes 26417152 | tf_op jit(solution)/shard_map/transpose(jvp())/reduce_sum | solution.py:589
  475.4 4.5 bitcast_convert_fusion.3
  480.0 4.0 multiply_convert_fusion
  485.3 6.5 maximum_maximum_fusion.conv
  491.8 171.1 %grads.1 = (bf16[1024,1024]{1,0:T(8,128)(2,1)}, bf16[1024,4096]{1,0:T(8,128)(2,1)}, bf16[2,2,128,512]{3,2,1,0:T(8,128)(2,1)}, f32[40,1024]{1,0:T(8,128)}) custom-call(bf16[4,1024,1024]{2,1,0:T(8,128)(2,1)} %get-tuple-element.21.s1, bf16[4,128,1024]{2,1,0:T(8,128)(2,1)} %get-tuple-element.22.f2, bf16[2,2,2,2,256,1024]{5,4,3,2,1,0:T(8,128)(2,1)} %maximum_maximum_fusion.conv, ...), custom_call_target="tpu_custom_call" | custom-call | tf_op jit(solution)/shard_map/grads/pallas_call | solution.py:526
  662.9 11.9 %convert_element_type.554 = f32[1024,4096]{1,0:T(8,128)} convert(bf16[1024,4096]{1,0:T(8,128)(2,1)} %get-tuple-element.27) | non-fusion elementwise | flops 4194304 | bytes 25165824 | tf_op jit(solution)/shard_map/convert_element_type | solution.py:910
  (446 shorter events, 104.3 us)
Async XLA Ops:
  2.2 36.3 %copy-start.32 = (f32[4,12,24]{2,1,0:T(8,128)}, f32[4,12,24]{2,1,0:T(8,128)S(1)}, u32[]{:S(2)}) copy-start(f32[4,12,24]{2,1,0:T(8,128)S(1)} %and_convert_fusion) | copy-start | bytes 13828
  9.3 20.8 %copy-start.108 = (f32[1,1,1024]{2,0,1:T(1,128)}, f32[1,1,1024]{2,0,1:T(1,128)S(1)}, u32[]{:S(2)}) copy-start(f32[1,1,1024]{2,0,1:T(1,128)S(1)} %get-tuple-element.149) | copy-start | bytes 12292
  9.3 29.1 %copy-start.86 = (f32[1,1,1024]{2,0,1:T(1,128)}, f32[1,1,1024]{2,0,1:T(1,128)S(1)}, u32[]{:S(2)}) copy-start(f32[1,1,1024]{2,0,1:T(1,128)S(1)} %get-tuple-element.148) | copy-start | bytes 12292
  9.3 48.6 %copy-start.80 = (f32[1,1,1024]{2,0,1:T(1,128)}, f32[1,1,1024]{2,0,1:T(1,128)S(1)}, u32[]{:S(2)}) copy-start(f32[1,1,1024]{2,0,1:T(1,128)S(1)} %get-tuple-element.147) | copy-start | bytes 12292
  10.0 20.2 %copy-start.151 = (f32[1,1,1024]{2,0,1:T(1,128)}, f32[1,1,1024]{2,0,1:T(1,128)S(1)}, u32[]{:S(2)}) copy-start(f32[1,1,1024]{2,0,1:T(1,128)S(1)} %get-tuple-element.155) | copy-start | bytes 12292
  10.0 28.5 %copy-start.124 = (f32[1,1,1024]{2,0,1:T(1,128)}, f32[1,1,1024]{2,0,1:T(1,128)S(1)}, u32[]{:S(2)}) copy-start(f32[1,1,1024]{2,0,1:T(1,128)S(1)} %get-tuple-element.154) | copy-start | bytes 12292
  10.0 48.0 %copy-start.110 = (f32[1,1,1024]{2,0,1:T(1,128)}, f32[1,1,1024]{2,0,1:T(1,128)S(1)}, u32[]{:S(2)}) copy-start(f32[1,1,1024]{2,0,1:T(1,128)S(1)} %get-tuple-element.153) | copy-start | bytes 12292
  12.0 7.8 %collective-permute-start = (bf16[4,1,24,1024]{3,2,1,0:T(8,128)(2,1)S(1)}, bf16[4,1,24,1024]{3,2,1,0:T(8,128)(2,1)S(1)}, u32[]{:S(2)}, u32[]{:S(2)}) collective-permute-start(bf16[4,1,24,1024]{3,2,1,0:T(8,128)(2,1)S(1)} %get-tuple-element.114), channel_id=1, source_target_pairs={{0,1},{2,3},{4,5},{6,7},{8,9},{10,11},{12,13},{14,15},{16,17},{18,... | collective-permute-start | bytes 589832 | tf_op jit(solution)/shard_map/ppermute | solution.py:576
  15.2 7.3 %collective-permute-start.1 = (bf16[4,1,24,1024]{3,2,1,0:T(8,128)(2,1)S(1)}, bf16[4,1,24,1024]{3,2,1,0:T(8,128)(2,1)S(1)}, u32[]{:S(2)}, u32[]{:S(2)}) collective-permute-start(bf16[4,1,24,1024]{3,2,1,0:T(8,128)(2,1)S(1)} %get-tuple-element.115), channel_id=1, source_target_pairs={{1,0},{3,2},{5,4},{7,6},{9,8},{11,10},{13,12},{15,14},{17,16},{19,... | collective-permute-start | bytes 589832 | tf_op jit(solution)/shard_map/ppermute | solution.py:578
  17.5 35.4 %copy-start.128 = (s32[4,12]{1,0:T(4,128)}, s32[4,12]{1,0:T(4,128)S(1)}, u32[]{:S(2)}) copy-start(s32[4,12]{1,0:T(4,128)S(1)} %get-tuple-element.160) | copy-start | bytes 580
  17.6 35.4 %copy-start.130 = (f32[4,12]{1,0:T(4,128)}, f32[4,12]{1,0:T(4,128)S(1)}, u32[]{:S(2)}) copy-start(f32[4,12]{1,0:T(4,128)S(1)} %get-tuple-element.161) | copy-start | bytes 580
  17.6 35.4 %copy-start.132 = (s32[4,12]{1,0:T(4,128)}, s32[4,12]{1,0:T(4,128)S(1)}, u32[]{:S(2)}) copy-start(s32[4,12]{1,0:T(4,128)S(1)} %get-tuple-element.165) | copy-start | bytes 580
  19.7 24.1 %copy-start.63 = (s32[4,6]{1,0:T(4,128)}, s32[4,6]{1,0:T(4,128)S(1)}, u32[]{:S(2)}) copy-start(s32[4,6]{1,0:T(4,128)S(1)} %get-tuple-element.162) | copy-start | bytes 292
  19.7 24.1 %copy-start.65 = (f32[4,6]{1,0:T(4,128)}, f32[4,6]{1,0:T(4,128)S(1)}, u32[]{:S(2)}) copy-start(f32[4,6]{1,0:T(4,128)S(1)} %get-tuple-element.163) | copy-start | bytes 292
  19.7 24.1 %copy-start.67 = (s32[4,6]{1,0:T(4,128)}, s32[4,6]{1,0:T(4,128)S(1)}, u32[]{:S(2)}) copy-start(s32[4,6]{1,0:T(4,128)S(1)} %get-tuple-element.164) | copy-start | bytes 292
  19.8 24.0 %copy-start.61 = (s32[4,12]{1,0:T(4,128)}, s32[4,12]{1,0:T(4,128)S(1)}, u32[]{:S(2)}) copy-start(s32[4,12]{1,0:T(4,128)S(1)} %broadcast_subtract_fusion) | copy-start | bytes 580
  59.8 11.9 %collective-permute-start.2 = (bf16[4,1,12,1024]{3,2,1,0:T(8,128)(2,1)S(1)}, bf16[4,1,12,1024]{3,2,1,0:T(8,128)(2,1)S(1)}, u32[]{:S(2)}, u32[]{:S(2)}) collective-permute-start(bf16[4,1,12,1024]{3,2,1,0:T(8,128)(2,1)S(1)} %get-tuple-element.120), channel_id=1, source_target_pairs={{0,1},{2,3},{4,5},{6,7},{8,9},{10,11},{12,13},{14,15},{16,17},{18,... | collective-permute-start | bytes 294920 | tf_op jit(solution)/shard_map/ppermute | solution.py:576
  61.1 10.6 %collective-permute-start.3 = (bf16[4,1,12,1024]{3,2,1,0:T(8,128)(2,1)S(1)}, bf16[4,1,12,1024]{3,2,1,0:T(8,128)(2,1)}, u32[]{:S(2)}, u32[]{:S(2)}) collective-permute-start(bf16[4,1,12,1024]{3,2,1,0:T(8,128)(2,1)S(1)} %get-tuple-element.121), channel_id=1, source_target_pairs={{1,0},{3,2},{5,4},{7,6},{9,8},{11,10},{13,12},{15,14},{17,16},{19,... | collective-permute-start | bytes 294920 | tf_op jit(solution)/shard_map/ppermute | solution.py:578
  379.8 19.3 %collective-permute-start.4 = (bf16[4,1,12,1024]{3,2,1,0:T(8,128)(2,1)S(1)}, bf16[4,1,12,1024]{3,2,1,0:T(8,128)(2,1)S(1)}, u32[]{:S(2)}, u32[]{:S(2)}) collective-permute-start(bf16[4,1,12,1024]{3,2,1,0:T(8,128)(2,1)S(1)} %get-tuple-element.118), channel_id=1, source_target_pairs={{0,1},{2,3},{4,5},{6,7},{8,9},{10,11},{12,13},{14,15},{16,17},{18,... | collective-permute-start | bytes 294920 | tf_op jit(solution)/shard_map/ppermute | solution.py:576
  384.1 15.0 %collective-permute-start.5 = (bf16[4,1,12,1024]{3,2,1,0:T(8,128)(2,1)S(1)}, bf16[4,1,12,1024]{3,2,1,0:T(8,128)(2,1)S(1)}, u32[]{:S(2)}, u32[]{:S(2)}) collective-permute-start(bf16[4,1,12,1024]{3,2,1,0:T(8,128)(2,1)S(1)} %get-tuple-element.119), channel_id=1, source_target_pairs={{1,0},{3,2},{5,4},{7,6},{9,8},{11,10},{13,12},{15,14},{17,16},{19,... | collective-permute-start | bytes 294920 | tf_op jit(solution)/shard_map/ppermute | solution.py:578
  410.4 16.7 %slice-start = ((s8[4718592]{0:T(1024)(128)(4,1)}), s8[4194304]{0:T(1024)(128)(4,1)S(1)}, s32[]{:S(2)}) async-start(s8[4718592]{0:T(1024)(128)(4,1)} %bitcast.206), calls=%async_computation | async-start | bytes 8388608
  450.5 8.6 %collective-permute-start.6 = (bf16[4,1,24,1024]{3,2,1,0:T(8,128)(2,1)S(1)}, bf16[4,1,24,1024]{3,2,1,0:T(8,128)(2,1)S(1)}, u32[]{:S(2)}, u32[]{:S(2)}) collective-permute-start(bf16[4,1,24,1024]{3,2,1,0:T(8,128)(2,1)S(1)} %get-tuple-element.112), channel_id=1, source_target_pairs={{0,1},{2,3},{4,5},{6,7},{8,9},{10,11},{12,13},{14,15},{16,17},{18,... | collective-permute-start | bytes 589832 | tf_op jit(solution)/shard_map/ppermute | solution.py:576
  454.5 7.0 %collective-permute-start.7 = (bf16[4,1,24,1024]{3,2,1,0:T(8,128)(2,1)S(1)}, bf16[4,1,24,1024]{3,2,1,0:T(8,128)(2,1)S(1)}, u32[]{:S(2)}, u32[]{:S(2)}) collective-permute-start(bf16[4,1,24,1024]{3,2,1,0:T(8,128)(2,1)S(1)} %get-tuple-element.113), channel_id=1, source_target_pairs={{1,0},{3,2},{5,4},{7,6},{9,8},{11,10},{13,12},{15,14},{17,16},{19,... | collective-permute-start | bytes 589832 | tf_op jit(solution)/shard_map/ppermute | solution.py:578
  662.9 16.2 %copy-start.44 = (bf16[2,2,128,512]{3,2,1,0:T(8,128)(2,1)S(1)}, bf16[2,2,128,512]{3,2,1,0:T(8,128)(2,1)}, u32[]{:S(2)}) copy-start(bf16[2,2,128,512]{3,2,1,0:T(8,128)(2,1)} %get-tuple-element.24) | copy-start | bytes 1572868
  (149 other events, 642.5 us)

commit v2 on v1

--- a/solution.py
+++ b/solution.py
@@ -118,15 +118,207 @@
     return v * phi, phi + v * dense * 0.3989422804014327
 
 
+def normal(v):
+    centred = v - jnp.mean(v, axis=-1, keepdims=True)
+    scale = lax.rsqrt(jnp.mean(centred * centred, axis=-1, keepdims=True) + 1e-06)
+    return centred * scale, scale
+
+
+def sigmoid(v):
+    return 1.0 / (1.0 + jnp.exp(-v))
+
+
+def silu_of(v):
+    return v * sigmoid(v)
+
+
+def column_masks(cmask, width):
+    place = lax.rem(lax.broadcasted_iota(jnp.int32, cmask.shape[1:], 0), width)
+    cmask[0] = jnp.where(place != 0, 1.0, 0.0)
+    cmask[1] = jnp.where(place != width - 1, 1.0, 0.0)
+
+
+def windows(cells, rim, first, masks):
+    middle = jnp.concatenate([rim * (1.0 - first), cells, rim * first], axis=0)
+    count = middle.shape[0]
+    left, right = pltpu.roll(middle, 1, 0), pltpu.roll(middle, count - 1, 0)
+    if masks is not None:
+        left, right = left * masks[0], right * masks[1]
+    return left, middle, right
+
+
+class Geometry:
+    def __init__(self, count, height, width):
+        self.count, self.height, self.width = count, height, width
+        self.cells = height * width
+
+    def rows(self, g):
+        return rows_of(g * self.cells, self.cells, 16)
+
+
+def head_stage(shape, per, x_of, w, gains, biases, mask, pre, hidden, rim_send, first):
+    cells = shape.cells * per
+
+    def body(i, carry):
+        rows = rows_of(i * cells, cells, 16)
+        x = x_of(rows)
+        value = nn(x, w[...])
+        pre[rows] = value.astype(BF)
+        n, _ = normal(value)
+        h = silu_of(n * gains[0:1] + biases[0:1]) * mask[rows]
+        hidden[rows] = h.astype(BF)
+        for g in range(per):
+            at = g * shape.cells
+            top = h[at : at + shape.width]
+            bottom = h[at + shape.cells - shape.width : at + shape.cells]
+            rim_send[i * per + g, pl.ds(0, shape.width)] = (bottom * first + top * (1.0 - first)).astype(BF)
+        return carry
+
+    lax.fori_loop(0, shape.count // per, body, 0)
+
+
+def depth_stage(shape, hidden, rim, taps, cmask, pre, first, channels):
+    def body(i, carry):
+        g, l = i // (channels // 128), lax.rem(i, channels // 128)
+        rows, lanes = shape.rows(g), rows_of(l * 128, 128, 128)
+        shifted = windows(
+            hidden[rows, lanes].astype(F32),
+            rim[g, pl.ds(0, shape.width), lanes].astype(F32),
+            first,
+            None if cmask is None else (cmask[0], cmask[1]),
+        )
+        total = jnp.zeros((shape.cells, 128), F32)
+        for a in range(3):
+            for b in range(3):
+                piece = shifted[b][a * shape.width : a * shape.width + shape.cells]
+                total = total + piece * taps[3 * a + b : 3 * a + b + 1, lanes]
+        pre[rows, lanes] = total.astype(BF)
+        return carry
+
+    lax.fori_loop(0, shape.count * (channels // 128), body, 0)
+
+
+def tail_stage(shape, per, x, w, gains, biases, mask, pre_two, pre_three, result):
+    cells = shape.cells * per
+
+    def body(i, carry):
+        rows = rows_of(i * cells, cells, 16)
+        n, _ = normal(pre_two[rows].astype(F32))
+        h = (silu_of(n * gains[1:2] + biases[1:2]) * mask[rows]).astype(BF)
+        value = nn(h, w[...])
+        pre_three[rows] = value.astype(BF)
+        n, _ = normal(value)
+        out = silu_of(x[rows].astype(F32) + n * gains[2:3] + biases[2:3]) * mask[rows]
+        result(i, rows, out)
+        return carry
+
+    lax.fori_loop(0, shape.count // per, body, 0)
+
+
+def slope_of(v, s):
+    return s * (1.0 + v * (1.0 - s))
+
+
+def norm_back(n, scale, grad, gain, sums, at):
+    sums[at : at + 1] += jnp.sum(grad * n, axis=0, keepdims=True)
+    sums[at + 3 : at + 4] += jnp.sum(grad, axis=0, keepdims=True)
+    dn = grad * gain
+    return scale * (dn - jnp.mean(dn, axis=-1, keepdims=True) - n * jnp.mean(dn * n, axis=-1, keepdims=True))
+
+
+def back_tail_stage(shape, per, grad_of, x, w, gains, biases, mask, pre_two, pre_three, resid, third, hidden_two, second, edge, first, sums, base):
+    cells = shape.cells * per
+
+    def body(i, carry):
+        rows = rows_of(i * cells, cells, 16)
+        live = mask[rows]
+        n, scale = normal(pre_three[rows].astype(F32))
+        v = x[rows].astype(F32) + n * gains[2:3] + biases[2:3]
+        grad = grad_of(i) * slope_of(v, sigmoid(v)) * live
+        resid[rows] = grad.astype(BF)
+        low = norm_back(n, scale, grad, gains[2:3], sums, base + 11).astype(BF)
+        third[rows] = low
+        grad = nt(low, w[...])
+        n, scale = normal(pre_two[rows].astype(F32))
+        v = n * gains[1:2] + biases[1:2]
+        s = sigmoid(v)
+        hidden_two[rows] = (v * s * live).astype(BF)
+        grad = norm_back(n, scale, grad * live * slope_of(v, s), gains[1:2], sums, base + 10)
+        second[rows] = grad.astype(BF)
+        for g in range(per):
+            at = g * shape.cells
+            top = grad[at : at + shape.width]
+            bottom = grad[at + shape.cells - shape.width : at + shape.cells]
+            edge[i * per + g, pl.ds(0, shape.width)] = (bottom * first + top * (1.0 - first)).astype(BF)
+        return carry
+
+    lax.fori_loop(0, shape.count // per, body, 0)
+
+
+def back_depth_stage(shape, second, rim, hidden, hidden_rim, taps, cmask, result, first, channels, sums, base):
+    masks = None if cmask is None else (cmask[0], cmask[1])
+
+    def body(i, carry):
+        g, l = i // (channels // 128), lax.rem(i, channels // 128)
+        rows, lanes = shape.rows(g), rows_of(l * 128, 128, 128)
+        edge = pl.ds(0, shape.width)
+        grad = second[rows, lanes].astype(F32)
+        shifted = windows(grad, rim[g, edge, lanes].astype(F32), first, masks)
+        total = jnp.zeros((shape.cells, 128), F32)
+        for a in range(3):
+            for b in range(3):
+                at = (2 - a) * shape.width
+                total = total + shifted[2 - b][at : at + shape.cells] * taps[3 * a + b : 3 * a + b + 1, lanes]
+        result[rows, lanes] = total.astype(BF)
+        shifted = windows(hidden[rows, lanes].astype(F32), hidden_rim[g, edge, lanes].astype(F32), first, masks)
+        for a in range(3):
+            for b in range(3):
+                at = a * shape.width
+                line = base + 3 * a + b
+                sums[line : line + 1, lanes] += jnp.sum(
+                    grad * shifted[b][at : at + shape.cells], axis=0, keepdims=True
+                )
+        return carry
+
+    lax.fori_loop(0, shape.count * (channels // 128), body, 0)
+
+
+def back_head_stage(shape, per, one_grad, w, gains, biases, mask, pre_one, resid, first_low, result, sums, base):
+    cells = shape.cells * per
+
+    def body(i, carry):
+        rows = rows_of(i * cells, cells, 16)
+        n, scale = normal(pre_one[rows].astype(F32))
+        v = n * gains[0:1] + biases[0:1]
+        grad = one_grad[rows].astype(F32) * mask[rows] * slope_of(v, sigmoid(v))
+        low = norm_back(n, scale, grad, gains[0:1], sums, base + 9).astype(BF)
+        first_low[rows] = low
+        result(i, rows, resid[rows].astype(F32) + nt(low, w[...]))
+        return carry
+
+    lax.fori_loop(0, shape.count // per, body, 0)
+
+
+def outer_stage(left, right, out):
+    high = out.shape[2]
+
+    def body(i, carry):
+        at = rows_of(i * high, high, 128)
+        out[i // 2, lax.rem(i, 2)] = tn(left[:, at], right[...]).astype(BF)
+        return carry
+
+    lax.fori_loop(0, out.shape[0] * 2, body, 0)
+
+
 def readout_kernel(
-    nz, ndp, nrow,
-    mine, cot, rin_part, rout_part, bias_part, bias_out,
-    tokens, agrad, s1, f2, hsum, rc2, rp2,
-    rin, rout, bias, abst, abst_t, hid, mg, ag_send, ag_recv, s2, send, recv, local,
+    nz, ndp, nrow, zero, one,
+    patches, cot, rin_part, rout_part, bias_part, bias_out, conv_in, conv_out, taps, gains, biases, mask_zero, mask_one, pool, pick,
+    tokens, agrad, s1, f2, hsum, rc1, rc2, rp2, keep_zero, keep_one, rim_zero, rim_one,
+    rin, rout, bias, abst, abst_t, hid, mg, ag_send, ag_recv, s2, cmask, edge_zero, edge_one, send, recv, local,
 ):
     me = Place(nz, ndp, nrow)
     links = Links(send, recv)
-    T, C = mine.shape
+    T, C = agrad.shape
     hw, ow = rout.shape[1], rout.shape[2]
     tall = nz * T
     np_ = 2 * me.nq
@@ -137,10 +329,15 @@
     own = [
         pltpu.make_async_copy(rin_part, rin.at[0], local.at[0]),
         pltpu.make_async_copy(rout_part.at[:, rows_of(me.k * ow, ow, 128)], rout.at[0], local.at[1]),
-        pltpu.make_async_copy(mine, abst.at[rows_of(me.k * T, T, 16)], local.at[2]),
     ]
-    for copy in own:
-        copy.start()
+    convs = [
+        pltpu.make_async_copy(part.at[b], s2.at[2 * b + i], local.at[2 + 2 * b + i])
+        for b in range(2)
+        for i, part in enumerate((conv_in, conv_out))
+    ]
+    given = pltpu.make_async_copy(patches, mg.at[0], local.at[6])
+    convs[0].start()
+    given.start()
     za, zb, zc = [], [], []
     row_a = rows_of(strip * ra, ra, ra)
     row_b = rows_of(strip * rb, rb, rb)
@@ -150,17 +347,17 @@
         zc.append(links.copy(bias_part, bias.at[t], me.at(k=there)))
     start_all(za)
     start_all(zc)
-    here = rows_of(me.k * T, T, 16)
-    zg = [links.copy(mine, abst.at[here], me.at(k=lax.rem(me.k + nz - t, nz))) for t in range(1, nz)]
-    start_all(zg)
     for t in range(1, nz):
         there = lax.rem(me.k + nz - t, nz)
         zb.append(links.copy(
             rout_part.at[row_b, rows_of(there * ow, ow, 128)], rout.at[t, row_b], me.at(k=there)))
     start_all(zb)
+    for copy in convs[1:] + own:
+        copy.start()
     bias[0] = bias_part[...]
-
-    def across(weights, row, height, arrived):
+    column_masks(cmask, zero.width)
+
+    def across(weights, row, arrived):
         recv_all(arrived)
         part = weights.at[pl.ds(1, nz - 1), row]
         return start_all([links.copy(part, part, me.at(q=me.chip(t))) for t in range(1, me.nq)])
@@ -171,11 +368,54 @@
         part = weights.at[pl.ds(1, nz - 1), half]
         return start_all([links.copy(part, part, me.at(c=1 - me.c))])
 
-    pa = across(rin, row_a, ra, za)
-    pb = across(rout, row_b, rb, zb)
+    first = (1 - me.r).astype(F32)
+    neighbour = me.at(q=me.x * nrow + (nrow - 1 - me.r))
+
+    def masked(rows):
+        x = (mg[0, rows].astype(F32) * mask_zero[rows]).astype(BF)
+        mg[0, rows] = x
+        return x
+
+    convs[0].wait()
+    given.wait()
+    head_stage(zero, 1, masked, s2.at[0], gains.at[0], biases.at[0], mask_zero, hid.at[0], hid.at[1], edge_zero, first)
+    rim0 = links.copy(edge_zero, rim_zero, neighbour)
+    rim0.start()
+    pa = across(rin, row_a, za)
+    rim0.wait_recv()
+    depth_stage(zero, hid.at[1], rim_zero, taps.at[0], cmask, hid.at[2], first, C)
+    for copy in convs[1:]:
+        copy.wait()
+
+    def to_pooled(i, rows, out):
+        mg[1, one.rows(i)] = nn(pool[i], out.astype(BF)).astype(BF)
+
+    tail_stage(zero, 1, mg.at[0], s2.at[1], gains.at[0], biases.at[0], mask_zero, hid.at[2], hid.at[3], to_pooled)
+    kept_zero = pltpu.make_async_copy(hid, keep_zero, local.at[2])
+    kept_zero.start()
+    all_one = one.cells * one.count
+    part = [mg.at[1 + i // 3, pl.ds((i % 3) * all_one, all_one)] for i in range(5)]
+    pooled, pre_one, hidden, pre_two, pre_three = part
+    head_stage(one, one.count, lambda rows: pooled[rows], s2.at[2], gains.at[1], biases.at[1], mask_one, pre_one, hidden, edge_one, first)
+    rim1 = links.copy(edge_one, rim_one, neighbour)
+    rim1.start()
+    pb = across(rout, row_b, zb)
+    rim1.wait_recv()
+    depth_stage(one, hidden, rim_one, taps.at[1], None, pre_two, first, C)
+    here = rows_of(me.k * T, T, 16)
+
+    def to_tokens(i, rows, out):
+        abst[here] = nn(pick[...], out.astype(BF)).astype(BF)
+
+    tail_stage(one, one.count, pooled, s2.at[3], gains.at[1], biases.at[1], mask_one, pre_two, pre_three, to_tokens)
+    kept_one = pltpu.make_async_copy(mg.at[pl.ds(1, 2)], keep_one, local.at[3])
+    kept_one.start()
+    zg = start_all([
+        links.copy(abst.at[here], abst.at[here], me.at(k=lax.rem(me.k + nz - t, nz))) for t in range(1, nz)
+    ])
     ca = between_cores(rin, ra, pa)
     cb = between_cores(rout, rb, pb)
-    for copy in own:
+    for copy in own + [kept_zero, kept_one]:
         copy.wait()
     recv_all(zc)
     recv_all(ca)
@@ -239,15 +479,20 @@
     theirs = rows_of((1 - me.c) * half, half, half)
     core2 = start_all([links.copy(s2.at[:, theirs], rc2, me.at(c=1 - me.c))])
 
+    abst_t[...] = abst[...].T
+    sent_all(zg)
+
     def f2_body(i, carry):
         at = rows_of(i * 256, 256, 256)
         total = nn(hid[0], rout[0, :, at]) + bias_out[0:1, at]
         for u in range(1, nz):
             total = total + nn(hid[u], rout[u, :, at])
-        tokens[:, at] = total.astype(BF)
+        abst[:, at] = total.astype(BF)
         return carry
 
     lax.fori_loop(0, ow // 256, f2_body, 0)
+    out_tokens = pltpu.make_async_copy(abst, tokens, local.at[6])
+    out_tokens.start()
     recv_all(core2)
     sent_all(core2)
     loads = [
@@ -269,7 +514,6 @@
         sends2.append(links.copy(src, rp2.at[t - 1], me.at(q=q)))
     start_all(sends2)
 
-    abst_t[...] = abst[...].T
 
     def g1(i, carry):
         u = i // (C // 256)
@@ -278,17 +522,29 @@
         return carry
 
     lax.fori_loop(0, nz * (C // 256), g1, 0)
-    outs = [
-        pltpu.make_async_copy(hid.at[u, pl.ds(0, C)], s1.at[me.deep(u)], local.at[2 + u]) for u in range(nz)
-    ]
-    for copy in outs:
-        copy.start()
+    low = me.nq * ra
+    core1 = links.copy(hid.at[:, rows_of((1 - me.c) * low, low, low)], rc1, me.at(c=1 - me.c))
+    core1.start()
     recv_all(ag[1:])
     fold(
         lambda at, v: agrad.__setitem__(at, v),
         [lambda at: agrad[at]] + [lambda at, t=t: ag_recv[t - 1, at] for t in range(1, nz)],
         T, 32,
     )
+    core1.wait_recv()
+    loads = [pltpu.make_async_copy(rc1.at[u], mg.at[u, pl.ds(0, low)], local.at[u]) for u in range(nz)]
+    for copy in loads:
+        copy.start()
+    outs = []
+    for u in range(nz):
+        loads[u].wait()
+        fold(
+            lambda at, v, u=u: hid.__setitem__((u, rows_of(me.c * low + at.start, at.size, 16)), v.astype(BF)),
+            [lambda at, u=u: hid[u, rows_of(me.c * low + at.start, at.size, 16)], lambda at, u=u: mg[u, at]],
+            low, 32,
+        )
+        outs.append(pltpu.make_async_copy(hid.at[u, rows_of(me.c * low, low, low)], s1.at[u], local.at[u]))
+        outs[-1].start()
     for copy in outs:
         copy.wait()
     recv_all(sends2)
@@ -307,15 +563,18 @@
             + [lambda at, j=j, t=t: mg[j, rows_of(t * rb + at.start, at.size, 16)] for t in range(1, me.nq)],
             rb, min(rb, 32),
         )
-    for group_of in (za, zb, zc, zg, pa, pb, ca, cb, ag[1:], sends2):
+    out_tokens.wait()
+    for group_of in (za, zb, zc, pa, pb, ca, cb, ag[1:], sends2, [rim0, rim1, core1]):
         sent_all(group_of)
 
 
 def grads_kernel(
-    nz, ndp, nrow,
-    s1, f2, conv, small,
-    out1, out2, out3, small_out,
-    m1, rc1, rp1, f1, rz1, m3, rc3, rp3, f3, rz3, sc, sp, sz, send, recv, local,
+    nz, ndp, nrow, zero, one,
+    s1, f2, agrad, patches, keep_zero, keep_one, rim_zero, rim_one, conv_in, conv_out, taps, gains, biases,
+    mask_zero, mask_one, pool, pick, small_in,
+    out1, out2, out3, small, patch_grad, rp1,
+    xs, kept, keep, third, resid, weights, cmask, edge_zero, edge_one, got_zero, got_one,
+    f1, rz1, conv, rc3, rp3, f3, rz3, sc, sp, sz, send, recv, local,
 ):
     me = Place(nz, ndp, nrow)
     links = Links(send, recv)
@@ -327,111 +586,178 @@
     width = C // nrow
     R = out3.shape[2] // 2
     other = me.at(c=1 - me.c)
-    half = me.nq * ra
+    first = (1 - me.r).astype(F32)
+    neighbour = me.at(q=me.x * nrow + (nrow - 1 - me.r))
     me.greet()
 
-    sums = start_all([links.copy(small, sc, other)])
-    theirs = rows_of((1 - me.c) * half, half, half)
-    core3 = [links.copy(conv.at[b, :, :, 1 - me.c], rc3.at[b], other) for b in range(2)]
-    core1 = links.copy(s1.at[:, theirs], rc1, other)
-    core1.start()
-    start_all(core3)
+    loads = [
+        pltpu.make_async_copy(keep_one, keep, local.at[0]),
+        pltpu.make_async_copy(conv_out.at[1], weights.at[1], local.at[1]),
+        pltpu.make_async_copy(conv_in.at[1], weights.at[0], local.at[2]),
+        pltpu.make_async_copy(keep_zero, kept, local.at[3]),
+        pltpu.make_async_copy(patches, xs, local.at[4]),
+    ]
+    for copy in loads:
+        copy.start()
+    p1 = start_all([
+        links.copy(s1.at[:, rows_of(me.chip(t) * ra, ra, ra)], rp1.at[t - 1], me.at(q=me.chip(t)))
+        for t in range(1, me.nq)
+    ])
     row_b = rows_of(strip * rb, rb, rb)
     col_k = rows_of(me.k * ow, ow, 128)
     z2 = start_all([
         links.copy(f2.at[me.deep(t)], out2.at[row_b, col_k], me.at(k=me.deep(t))) for t in range(1, nz)
     ])
-    own = [
-        pltpu.make_async_copy(s1.at[:, rows_of(me.c * half, half, half)], m1, local.at[0]),
-        pltpu.make_async_copy(conv.at[0, :, :, me.c], m3.at[0], local.at[1]),
-        pltpu.make_async_copy(conv.at[1, :, :, me.c], m3.at[1], local.at[2]),
-    ]
-    for copy in own:
-        copy.start()
-    out2[row_b, col_k] = f2[me.k]
-    recv_all(sums)
-    sent_all(sums)
-    small_out[...] = small[...] + sc[...]
-    sums_p = start_all([links.copy(small_out, sp.at[t - 1], me.at(q=me.chip(t))) for t in range(1, me.nq)])
-
-    for copy in own:
-        copy.wait()
-    core1.wait_recv()
-    for j in range(nz):
-        fold(
-            lambda at, v, j=j: m1.__setitem__((j, at), v.astype(BF)),
-            [lambda at, j=j: m1[j, at], lambda at, j=j: rc1[j, at]],
-            half, 32,
-        )
-    p1 = start_all([
-        links.copy(m1.at[:, rows_of(me.chip(t) * ra, ra, ra)], rp1.at[t - 1], me.at(q=me.chip(t)))
-        for t in range(1, me.nq)
-    ])
-    p3 = []
-    for b in range(2):
+    own2 = pltpu.make_async_copy(f2.at[me.k], out2.at[row_b, col_k], local.at[5])
+    own2.start()
+    small[...] = jnp.zeros_like(small)
+    small[32:40] = small_in[...]
+    column_masks(cmask, zero.width)
+
+    def spread(b):
         core3[b].wait_recv()
         for m in range(2):
             for x in range(me.nx):
                 fold(
-                    lambda at, v, i=(b, m, x): m3.__setitem__((*i, at), v.astype(BF)),
-                    [lambda at, i=(b, m, x): m3[(*i, at)], lambda at, i=(b, m, x): rc3[(*i, at)]],
+                    lambda at, v, i=(b, m, x, me.c): conv.__setitem__((*i, at), v.astype(BF)),
+                    [lambda at, i=(b, m, x, me.c): conv[(*i, at)], lambda at, i=(b, m, x): rc3[(*i, at)]],
                     nz * R, 32,
                 )
         sends = []
         for t in range(1, me.nq):
             q = me.chip(t)
             cols = rows_of(lax.rem(q, nrow) * width, width, 128)
-            sends.append(links.copy(m3.at[b, :, q // nrow, :, cols], rp3.at[b, t - 1], me.at(q=q)))
-        p3.append(start_all(sends))
-
+            sends.append(links.copy(conv.at[b, :, q // nrow, me.c, :, cols], rp3.at[b, t - 1], me.at(q=q)))
+        return start_all(sends)
+
+    core3, p3 = [None, None], [None, None]
+
+    all_one = one.cells * one.count
+    pooled, pre_one, hidden, pre_two, pre_three, pooled_grad = [
+        keep.at[i // 3, pl.ds((i % 3) * all_one, all_one)] for i in range(6)
+    ]
+    third_one, resid_one = third.at[pl.ds(0, all_one)], resid.at[pl.ds(0, all_one)]
+    loads[0].wait()
+    loads[1].wait()
+    back_tail_stage(
+        one, one.count, lambda i: nn(pick[...], agrad[...].astype(BF)), pooled, weights.at[1], gains.at[1], biases.at[1], mask_one,
+        pre_two, pre_three, resid_one, third_one, pre_three, pre_two, edge_one, first, small, 16,
+    )
+    rim1 = links.copy(edge_one, got_one, neighbour)
+    rim1.start()
+    outer_stage(third_one, pre_three, conv.at[1, 1])
+    rim1.wait_recv()
+    back_depth_stage(one, pre_two, got_one, hidden, rim_one, taps.at[1], None, third_one, first, C, small, 16)
+    loads[2].wait()
+
+    def to_pooled_grad(i, rows, grad):
+        pooled_grad[rows] = grad.astype(BF)
+
+    back_head_stage(
+        one, one.count, third_one, weights.at[0], gains.at[1], biases.at[1], mask_one, pre_one, resid_one, pre_three, to_pooled_grad, small, 16
+    )
+    again = [
+        pltpu.make_async_copy(conv_out.at[0], weights.at[1], local.at[1]),
+        pltpu.make_async_copy(conv_in.at[0], weights.at[0], local.at[2]),
+    ]
+    for copy in again:
+        copy.start()
+    outer_stage(pre_three, pooled, conv.at[1, 0])
+    core3[1] = links.copy(conv.at[1, :, :, 1 - me.c], rc3.at[1], other)
+    core3[1].start()
+
+    loads[3].wait()
+    loads[4].wait()
+    xs[...] = (xs[...].astype(F32) * mask_zero[...]).astype(BF)
+    again[0].wait()
+    back_tail_stage(
+        zero, 1, lambda i: tn(pool[i], pooled_grad[one.rows(i)]), xs, weights.at[1], gains.at[0], biases.at[0], mask_zero,
+        kept.at[2], kept.at[3], resid, third, kept.at[3], kept.at[2], edge_zero, first, small, 0,
+    )
+    rim0 = links.copy(edge_zero, got_zero, neighbour)
+    rim0.start()
+    p3[1] = spread(1)
+    outer_stage(third, kept.at[3], conv.at[0, 1])
+    rim0.wait_recv()
+    back_depth_stage(zero, kept.at[2], got_zero, kept.at[1], rim_zero, taps.at[0], cmask, third, first, C, small, 0)
+    again[1].wait()
+
+    def to_patches(i, rows, grad):
+        resid[rows] = (grad * mask_zero[rows]).astype(BF)
+
+    back_head_stage(
+        zero, 1, third, weights.at[0], gains.at[0], biases.at[0], mask_zero, kept.at[0], resid, kept.at[3], to_patches, small, 0
+    )
+    out_patches = pltpu.make_async_copy(resid, patch_grad, local.at[0])
+    out_patches.start()
+    outer_stage(kept.at[3], xs, conv.at[0, 0])
+    core3[0] = links.copy(conv.at[0, :, :, 1 - me.c], rc3.at[0], other)
+    core3[0].start()
+    sums = start_all([links.copy(small, sc, other)])
+    p3[0] = spread(0)
+
+    own2.wait()
     recv_all(z2)
     g2 = start_all([
         links.copy(out2.at[row_b], out2.at[row_b], me.at(q=me.chip(t))) for t in range(1, me.nq)
     ])
-
-    sent_all(sums_p)
-    recv_all(sums_p)
-    for t in range(1, me.nq):
-        small_out[...] += sp[t - 1]
-    sums_z = start_all([links.copy(small_out, sz.at[t - 1], me.at(k=me.deep(t))) for t in range(1, nz)])
+    recv_all(sums)
+    sent_all(sums)
+    small[...] += sc[...]
+    sums_p = start_all([links.copy(small, sp.at[t - 1], me.at(q=me.chip(t))) for t in range(1, me.nq)])
 
     recv_all(p1)
-    mine = rows_of(me.q * ra, ra, ra)
+    pieces = [
+        pltpu.make_async_copy(
+            (s1.at[j, rows_of(me.q * ra, ra, ra)] if t == 0 else rp1.at[t - 1, j]), kept.at[t, pl.ds(j * ra, ra)], local.at[6 + t * nz + j]
+        )
+        for t in range(me.nq)
+        for j in range(nz)
+    ]
+    for copy in pieces:
+        copy.start()
+    for copy in pieces:
+        copy.wait()
     for j in range(nz):
         fold(
             lambda at, v, j=j: f1.__setitem__((j, at), v.astype(BF)),
-            [lambda at, j=j: m1[j, rows_of(me.q * ra + at.start, at.size, 16)]]
-            + [lambda at, j=j, t=t: rp1[t - 1, j, at] for t in range(1, me.nq)],
+            [lambda at, j=j, t=t: kept[t, rows_of(j * ra + at.start, at.size, 16)] for t in range(me.nq)],
             ra, 32,
         )
-    z1 = start_all([links.copy(f1.at[me.deep(t)], rz1.at[t - 1], me.at(k=me.deep(t))) for t in range(1, nz)])
-    z3 = []
+    z1 = start_all([links.copy(f1.at[t], rz1.at[t - 1], me.at(k=me.deep(t))) for t in range(1, nz)])
+    z3 = [None, None]
     my_cols = rows_of(me.r * width, width, 128)
-    for b in range(2):
+    for b in (1, 0):
         recv_all(p3[b])
         for m in range(2):
             for j in range(nz):
                 rows = pl.ds(j * R, R)
-                total = m3[b, m, me.x, rows, my_cols].astype(F32)
+                total = conv[b, m, me.x, me.c, rows, my_cols].astype(F32)
                 for t in range(1, me.nq):
                     total = total + rp3[b, t - 1, m, rows, :].astype(F32)
                 f3[b, j, pl.ds(m * R, R)] = total.astype(BF)
-        z3.append(start_all([
+        z3[b] = start_all([
             links.copy(f3.at[b, me.deep(t)], rz3.at[b, t - 1], me.at(k=me.deep(t))) for t in range(1, nz)
-        ]))
+        ])
+
+    sent_all(sums_p)
+    recv_all(sums_p)
+    for t in range(1, me.nq):
+        small[...] += sp[t - 1]
+    sums_z = start_all([links.copy(small, sz.at[t - 1], me.at(k=me.deep(t))) for t in range(1, nz)])
 
     recv_all(z1)
     row_a = rows_of(strip * ra, ra, ra)
     fold(
         lambda at, v: out1.__setitem__(rows_of(strip * ra + at.start, at.size, 16), v.astype(BF)),
-        [lambda at: f1[me.k, at]] + [lambda at, t=t: rz1[t - 1, at] for t in range(1, nz)],
+        [lambda at: f1[0, at]] + [lambda at, t=t: rz1[t - 1, at] for t in range(1, nz)],
         ra, 32,
     )
     g1 = start_all([
         links.copy(out1.at[row_a], out1.at[row_a], me.at(q=me.chip(t))) for t in range(1, me.nq)
     ])
     g3 = []
-    for b in range(2):
+    for b in (1, 0):
         recv_all(z3[b])
         total = f3[b, me.k].astype(F32)
         for t in range(1, nz):
@@ -445,16 +771,17 @@
     half_b = rows_of(me.c * me.nq * rb, me.nq * rb, me.nq * rb)
     h2 = start_all([links.copy(out2.at[half_b], out2.at[half_b], other)])
     recv_all(g1)
-    half_a = rows_of(me.c * half, half, half)
+    half_a = rows_of(me.c * me.nq * ra, me.nq * ra, me.nq * ra)
     h1 = start_all([links.copy(out1.at[half_a], out1.at[half_a], other)])
     sent_all(sums_z)
     recv_all(sums_z)
     for t in range(1, nz):
-        small_out[...] += sz[t - 1]
+        small[...] += sz[t - 1]
     recv_all(g3)
     recv_all(h1)
     recv_all(h2)
-    for group_of in ([core1], core3, z2, p1, p3[0], p3[1], g2, z1, z3[0], z3[1], g1, g3, h1, h2):
+    out_patches.wait()
+    for group_of in (core3, z2, p1, p3[0], p3[1], g2, z1, z3[0], z3[1], g1, g3, h1, h2, [rim0, rim1]):
         sent_all(group_of)
 
 
@@ -462,30 +789,35 @@
     return [pl.BlockSpec(memory_space=kind) for kind in kinds]
 
 
-def run_readout(mesh, token_rows, cot, read_in, read_out, read_bias):
+def run_readout(mesh, zero, one, patches, cot, read_in, read_out, read_bias, conv_in, conv_out, taps, gains, biases, masks, pool, pick):
     nz, ndp, nrow = mesh.shape["wide"], mesh.shape["dp"], mesh.shape["row"]
     nq = ndp // 2 * nrow
-    T, C = token_rows.shape
+    T, C = pick.shape[0], patches.shape[1]
     hw, ow = read_out.shape[0], cot.shape[1]
     tall = nz * T
     rb = hw // (2 * nq)
-    copies = 4 * (nz - 1) + 2 * (nq - 1) + 2 + (nz - 1) + 1 + (nq - 1)
+    copies = 4 * (nz - 1) + 2 * (nq - 1) + 2 + (nz - 1) + 1 + (nq - 1) + 3
     bias_part = jnp.broadcast_to(read_bias[0:1], (8, hw))
     bias_out = jnp.broadcast_to(read_bias[1:2], (8, ow))
     ANY = pl.ANY
     return pl.pallas_call(
-        functools.partial(readout_kernel, nz, ndp, nrow),
+        functools.partial(readout_kernel, nz, ndp, nrow, zero, one),
         out_shape=[
             jax.ShapeDtypeStruct((tall, ow), BF),
             jax.ShapeDtypeStruct((T, C), F32),
-            jax.ShapeDtypeStruct((nz, C, hw), BF),
+            jax.ShapeDtypeStruct((nz, C // 2, hw), BF),
             jax.ShapeDtypeStruct((nz, rb, ow), BF),
             jax.ShapeDtypeStruct((nz, 1, hw), F32),
+            jax.ShapeDtypeStruct((nz, C // 2, hw), BF),
             jax.ShapeDtypeStruct((nz, nq * rb, ow), BF),
             jax.ShapeDtypeStruct((nq - 1, nz, rb, ow), BF),
+            jax.ShapeDtypeStruct((4, tall, hw), BF),
+            jax.ShapeDtypeStruct((2, tall, hw), BF),
+            jax.ShapeDtypeStruct((zero.count, 32, C), BF),
+            jax.ShapeDtypeStruct((one.count, 16, C), BF),
         ],
-        in_specs=spec(ANY, VMEM, ANY, ANY, VMEM, VMEM),
-        out_specs=spec(VMEM, VMEM, ANY, VMEM, VMEM, ANY, ANY),
+        in_specs=spec(ANY, VMEM, ANY, ANY, VMEM, VMEM, ANY, ANY, VMEM, VMEM, VMEM, VMEM, VMEM, VMEM, VMEM),
+        out_specs=spec(ANY, VMEM, ANY, VMEM, VMEM, ANY, ANY, ANY, ANY, ANY, VMEM, VMEM),
         scratch_shapes=[
             VMEM((nz, C, hw), BF),
             VMEM((nz, hw, ow), BF),
@@ -497,49 +829,63 @@
             VMEM((nz - 1, T, C), BF),
             VMEM((nz - 1, T, C), BF),
             VMEM((nz, hw, ow), BF),
+            VMEM((2, zero.cells + 2 * zero.width, 128), F32),
+            VMEM((zero.count, 32, C), BF),
+            VMEM((one.count, 16, C), BF),
             pltpu.SemaphoreType.DMA((copies,)),
             pltpu.SemaphoreType.DMA((copies,)),
-            pltpu.SemaphoreType.DMA((nz + 2,)),
+            pltpu.SemaphoreType.DMA((7,)),
         ],
         compiler_params=pltpu.CompilerParams(
             collective_id=0, has_side_effects=True, vmem_limit_bytes=LIMIT
         ),
         name="readout",
-    )(token_rows, cot, read_in, read_out, bias_part, bias_out)
-
-
-LIMIT = 60 * 1024 * 1024
-
-
-def run_grads(mesh, s1, f2, conv, small):
+    )(patches, cot, read_in, read_out, bias_part, bias_out, conv_in, conv_out, taps, gains, biases, *masks, pool, pick)
+
+
+LIMIT = 62 * 1024 * 1024
+
+
+def run_grads(mesh, zero, one, s1, f2, agrad, patches, keep_zero, keep_one, rim_zero, rim_one, conv_in, conv_out, taps, gains, biases, masks, pool, pick, small_in):
     nz, ndp, nrow = mesh.shape["wide"], mesh.shape["dp"], mesh.shape["row"]
     nq = ndp // 2 * nrow
     nx = ndp // 2
-    _, C, hw = s1.shape
+    C, hw = s1.shape[1] * 2, s1.shape[2]
     _, rb, ow = f2.shape
     ra = C // (2 * nq)
     R = C // (ndp * nz)
-    S = small.shape[0]
-    copies = 3 + 1 + (nz - 1) + (nq - 1) * 2 + 2 * (nq - 1) + (nq - 1) + (nz - 1) * 2 + 2 * (nz - 1) + (nq - 1) + 2 * (nrow - 1) + 2
+    tall = patches.shape[0]
+    S = 40
+    copies = 1 + 2 + (nz - 1) + (nq - 1) * 2 + 2 * (nq - 1) + (nq - 1) + (nz - 1) * 2 + 2 * (nz - 1) + (nq - 1) + 2 * (nrow - 1) + 2 + 2
     width = C // nrow
     ANY = pl.ANY
     return pl.pallas_call(
-        functools.partial(grads_kernel, nz, ndp, nrow),
+        functools.partial(grads_kernel, nz, ndp, nrow, zero, one),
         out_shape=[
             jax.ShapeDtypeStruct((C, hw), BF),
             jax.ShapeDtypeStruct((hw, nz * ow), BF),
             jax.ShapeDtypeStruct((2, nrow, 2 * R, width), BF),
             jax.ShapeDtypeStruct((S, C), F32),
+            jax.ShapeDtypeStruct((tall, C), BF),
+            jax.ShapeDtypeStruct((nq - 1, nz, ra, hw), BF),
         ],
-        in_specs=spec(ANY, VMEM, ANY, VMEM),
-        out_specs=spec(VMEM, VMEM, VMEM, VMEM),
+        in_specs=spec(ANY, VMEM, VMEM, ANY, ANY, ANY, VMEM, VMEM, ANY, ANY, VMEM, VMEM, VMEM, VMEM, VMEM, VMEM, VMEM, VMEM),
+        out_specs=spec(VMEM, ANY, VMEM, VMEM, ANY, ANY),
         scratch_shapes=[
-            VMEM((nz, C // 2, hw), BF),
-            VMEM((nz, C // 2, hw), BF),
-            VMEM((nq - 1, nz, ra, hw), BF),
+            VMEM((tall, C), BF),
+            VMEM((4, tall, C), BF),
+            VMEM((2, tall, C), BF),
+            VMEM((tall, C), BF),
+            VMEM((tall, C), BF),
+            VMEM((2, C, C), BF),
+            VMEM((2, zero.cells + 2 * zero.width, 128), F32),
+            VMEM((zero.count, 32, C), BF),
+            VMEM((one.count, 16, C), BF),
+            VMEM((zero.count, 32, C), BF),
+            VMEM((one.count, 16, C), BF),
             VMEM((nz, ra, hw), BF),
             VMEM((nz - 1, ra, hw), BF),
-            VMEM((2, 2, nx, nz * R, C), BF),
+            VMEM((2, 2, nx, 2, nz * R, C), BF),
             VMEM((2, 2, nx, nz * R, C), BF),
             VMEM((2, nq - 1, 2, nz * R, width), BF),
             VMEM((2, nz, 2 * R, width), BF),
@@ -549,13 +895,13 @@
             VMEM((nz - 1, S, C), F32),
             pltpu.SemaphoreType.DMA((copies,)),
             pltpu.SemaphoreType.DMA((copies,)),
-            pltpu.SemaphoreType.DMA((3,)),
+            pltpu.SemaphoreType.DMA((6 + nq * nz,)),
         ],
         compiler_params=pltpu.CompilerParams(
             collective_id=1, has_side_effects=True, vmem_limit_bytes=LIMIT
         ),
         name="grads",
-    )(s1, f2, conv, small)
+    )(s1, f2, agrad, patches, keep_zero, keep_one, rim_zero, rim_one, conv_in, conv_out, taps, gains, biases, *masks, pool, pick, small_in)
 
 
 POOL = 12
@@ -648,7 +994,7 @@
     return (output, (flat_rows, first_pre, padded_one, second_pre, two_rows, third_pre))
 
 
-def block_backward(output_grad, source, live_mask, weights, kept, turned=False):
+def block_backward(output_grad, source, live_mask, weights, kept):
     w_first, w_last, tap_table, gain_rows, bias_rows = weights
     flat_rows, first_pre, padded_one, second_pre, two_rows, third_pre = kept
     grid_count, row_count, col_count, channels = source.shape
@@ -657,7 +1003,7 @@
     )
     residual_grad, third_grad, gain_three, bias_three = tail_back(output_grad)
     third_low = third_grad.astype(jnp.bfloat16).reshape(-1, channels)
-    grad_last = outer_sum(third_low, two_rows) if turned else outer_sum(two_rows, third_low)
+    grad_last = outer_sum(two_rows, third_low)
     two_grad = times_transposed(third_low, w_last).reshape(source.shape)
     _, middle_back = jax.vjp(
         functools.partial(head_piece, live_mask=live_mask), second_pre, gain_rows[1], bias_rows[1]
@@ -678,7 +1024,7 @@
     )
     first_grad, gain_one, bias_one = first_back(one_grad)
     first_low = first_grad.astype(jnp.bfloat16).reshape(-1, channels)
-    grad_first = outer_sum(first_low, flat_rows) if turned else outer_sum(flat_rows, first_low)
+    grad_first = outer_sum(flat_rows, first_low)
     source_grad = residual_grad + times_transposed(first_low, w_first).reshape(source.shape)
     grads = (
         grad_first,
@@ -839,10 +1185,6 @@
     )
     col_live = column_index[None, :] < grid_sizes[:, None]
     live_mask = (row_live[:, :, None] & col_live[:, None, :]).astype(jnp.float32)[..., None]
-    weights_one = (conv_in[0], conv_out[0], depth_taps[0], norm_gain[0], norm_bias[0])
-    weights_two = (conv_in[1], conv_out[1], depth_taps[1], norm_gain[1], norm_bias[1])
-    source = patches.astype(jnp.float32) * live_mask
-    encoded, kept_one = block_forward(source, live_mask, weights_one)
     pool_local = POOL // lax.axis_size("row")
     pooled_index = row_place * pool_local + jnp.arange(pool_local, dtype=jnp.int32)
     side_shaped = grid_sizes[:, None, None]
@@ -855,48 +1197,39 @@
         jnp.arange(POOL, dtype=jnp.int32)[None, :, None],
         column_index[None, None, :],
     )
-    pooled = jnp.einsum("gir,gjw,grwc->gijc", row_pool, col_pool, encoded, precision=exact_mode)
-    all_live = jnp.ones((grid_count, pool_local, POOL, 1), jnp.float32)
-    abstract, kept_two = block_forward(pooled, all_live, weights_two)
-    token_rows = abstract.astype(jnp.bfloat16).reshape(-1, channels)
+    zero = Geometry(grid_count, local_rows, grid_width)
+    one = Geometry(grid_count, pool_local, 16)
+    col_wide = jnp.pad(col_pool, ((0, 0), (0, one.width - POOL), (0, 0)))
+    pool = (row_pool[:, :, None, :, None] * col_wide[:, None, :, None, :]).reshape(grid_count, one.cells, zero.cells)
+    places = jnp.arange(grid_count * pool_local * POOL, dtype=jnp.int32)
+    places = places // POOL * one.width + places % POOL
+    pick = (places[:, None] == jnp.arange(grid_count * one.cells, dtype=jnp.int32)[None, :]).astype(BF)
+    mask_zero = live_mask.reshape(-1, 1)
+    mask_one = (jnp.arange(grid_count * one.cells, dtype=jnp.int32) % one.width < POOL).astype(F32)[:, None]
     cot_local = cotangent.reshape(-1, cotangent.shape[-1])
-    tokens, abstract_grad, s1, f2, hsum, _, _ = run_readout(
-        mesh, token_rows, cot_local, read_in, read_out, read_bias
+    shared = (conv_in, conv_out, depth_taps.astype(F32), norm_gain, norm_bias, (mask_zero, mask_one), pool.astype(BF))
+    flat = patches.reshape(-1, channels)
+    tokens, agrad, s1, f2, hsum, _, _, _, keep_zero, keep_one, rim_zero, rim_one = run_readout(
+        mesh, zero, one, flat, cot_local, read_in, read_out, read_bias, *shared, pick
     )
     tokens = tokens.reshape(cotangent.shape)
-    pooled_grad, grads_two = block_backward(
-        abstract_grad.reshape(abstract.shape), pooled, all_live, weights_two, kept_two, True
-    )
-    encoded_grad = jnp.einsum(
-        "gir,gjw,gijc->grwc", row_pool, col_pool, pooled_grad, precision=exact_mode
-    )
-    source_grad, grads_one = block_backward(encoded_grad, source, live_mask, weights_one, kept_one, True)
-    patch_grad = (source_grad * live_mask).astype(jnp.bfloat16)
-    R = channels // (ndp * nz)
-    conv = jnp.stack(
-        [jnp.stack([g[0].astype(BF), g[1].astype(BF)]) for g in (grads_one, grads_two)]
-    ).reshape(2, 2, ndp // 2, 2, nz * R, channels)
     cot_sum = jnp.sum(cot_local.astype(F32), axis=0)
     width = cot_sum.shape[0]
     cot_row = lax.dynamic_update_slice(
         jnp.zeros((nz * width,), F32), cot_sum, (lax.axis_index("wide") * width,)
     )
-    small = jnp.concatenate(
-        [piece for g in (grads_one, grads_two) for piece in g[2:]]
-        + [hsum.reshape(-1, channels), cot_row.reshape(-1, channels)]
-    )
-    lines = small.shape[0]
-    small = jnp.pad(small, ((0, -lines % 8), (0, 0)))
-    out1, out2, out3, small = run_grads(mesh, s1, f2, conv, small)
+    small = jnp.concatenate([hsum.reshape(-1, channels), cot_row.reshape(-1, channels)])
+    out1, out2, out3, small, patch_grad, _ = run_grads(
+        mesh, zero, one, s1, f2, agrad, flat, keep_zero, keep_one, rim_zero, rim_one, *shared, pick.T, small
+    )
+    patch_grad = patch_grad.reshape(patches.shape)
+    R = channels // (ndp * nz)
     out3 = out3.reshape(2, -1, 2, R, out3.shape[-1]).transpose(0, 2, 1, 4, 3).reshape(2, 2, channels, R).astype(F32)
     place = lax.axis_index("dp") * nz + lax.axis_index("wide")
     own = lax.dynamic_slice_in_dim(small, place * R, R, axis=1)
-    taps = jnp.stack([own[0:9], own[15:24]])
-    gains = jnp.stack([own[9:12], own[24:27]])
-    biases = jnp.stack([own[12:15], own[27:30]])
-    per = (lines - 30) // 2
-    flat = small[30:lines].reshape(2, per * channels)
-    bias_pair = lax.dynamic_slice_in_dim(flat, lax.axis_index("wide") * width, width, axis=1)
+    own = own[:32].reshape(2, 16, R)
+    taps, gains, biases = own[:, 0:9], own[:, 9:12], own[:, 12:15]
+    bias_pair = lax.dynamic_slice_in_dim(small[32:40].reshape(2, -1), lax.axis_index("wide") * width, width, axis=1)
     return (
         tokens,
         patch_grad,
@@ -912,7 +1245,7 @@
 
 
 def fits(mesh):
-    return mesh.shape["wide"] <= 4 and mesh.shape["dp"] % 2 == 0
+    return mesh.shape["wide"] == 4 and mesh.shape["dp"] % 2 == 0 and mesh.shape["row"] == 2
 
 
 def solution(mesh):

time: 694 us -> 565 us (0.81)
  other arithmetic: 97.1 us -> 25.6 us
  matrix products: 64.2 us -> 0 us
  Pallas kernels: 445 us -> 500 us
  local copies, waits for them, and re-layouts: 52.7 us -> 28.4 us
  starting transfers between devices: 18.6 us -> 0 us
    dot_general x16 -> x0, matrix products: 64.2 us -> none  [the longest x4 15.5 us: outer_sum(): lax.dot_general(left_rows, right_rows, (((0,), (0,)), ((), ())), preferre...]
    reduce_sum x20 -> x0, other arithmetic: 59.2 us -> none  [the longest x6 28.9 us: layer_norm(): return centred * lax.rsqrt(variance + eps_norm) * gain_row + bias_row]
    pallas_call x2, Pallas kernels: 445 us -> 500 us  [the longest x1 256 us: run_grads(): pl.pallas_call(functools.partial(grads_kernel, nz, ndp, nrow, zero, one),...]
    ppermute x8 -> x0, starting transfers between devices: 18.6 us -> none  [the longest x4 12.7 us: extended(): lax.ppermute(tail, axis, [(i, (i + 1) % count) for i in range(ends)])]
    unnamed x336 -> x13, local copies, waits for them, and re-layouts: 25.4 us -> 12.4 us
  transfers between devices with their start and end apart: 8 -> 0, of which waited for: 2 -> 0; matrix products, arithmetic and copies ran while one was open for 4% -> 0% of each run, Pallas kernels for 0% -> 0%
where the time goes in v2:
time: 565 us; the launch traced here: 556 us
  Pallas kernels  500 us (88%)
  local copies, waits for them, and re-layouts  28.4 us (5%)
  other arithmetic  25.6 us (5%)
    pallas_call x1, Pallas kernels, run_grads(): pl.pallas_call(functools.partial(grads_kernel, nz, ndp, nrow, zero, one),...  256 us
    pallas_call x1, Pallas kernels, run_readout(): pl.pallas_call(functools.partial(readout_kernel, nz, ndp, nrow, zero, one...  244 us
    unnamed x13, local copies, waits for them, and re-layouts  12.4 us
    convert_element_type x1, other arithmetic, on_device(): out2.astype(F32)  12 us

profile of v2, /device:TPU:17, one launch (start us, length us, event | category | flops | bytes accessed | tf_op | source)
XLA Modules:
  0.0 555.5 jit_solution(14228586745012259248)
XLA Ops:
  2.2 2.1 convert_reduce_fusion
  5.9 0.8 fusion.25
  8.4 1.4 copy.34.gains
  9.8 1.4 copy.35.biases
  11.1 1.4 copy_convert_fusion.taps
  13.2 0.8 fusion.1.pick
  14.0 0.8 fusion.pick
  14.8 1.0 reshape.556.mask_zero
  16.2 2.1 convert_element_type.85.pool
  18.3 3.0 copy.32
  21.3 2.1 reshape.546.cot
  23.4 244.0 %readout.1 = (bf16[1152,1024]{1,0:T(8,128)(2,1)}, f32[288,1024]{1,0:T(8,128)}, bf16[4,512,1024]{2,1,0:T(8,128)(2,1)}, bf16[4,128,1024]{2,1,0:T(8,128)(2,1)}, f32...) custom-call(bf16[1152,1024]{1,0:T(8,128)(2,1)} %bitcast.19, ...), custom_call_target="tpu_custom_call" | custom-call | tf_op jit(solution)/shard_map/readout/pallas_call | solution.py:803
  268.8 256.3 %grads.1 = (bf16[1024,1024]{1,0:T(8,128)(2,1)}, bf16[1024,4096]{1,0:T(8,128)(2,1)}, bf16[2,2,128,512]{3,2,1,0:T(8,128)(2,1)}, f32[40,1024]{1,0:T(8,128)}, bf16[1...) custom-call(bf16[4,512,1024]{2,1,0:T(8,128)(2,1)} %get-tuple-element.25.s1, ...), custom_call_target="tpu_custom_call" | custom-call | tf_op jit(solution)/shard_map/grads/pallas_call | solution.py:862
  525.1 0.8 constant_dynamic-slice_fusion.1
  525.9 0.8 slice.35
  529.1 1.2 convert_bitcast_fusion
  530.2 0.8 copy.40
  531.1 0.9 reshape.554
  532.0 1.0 slice_bitcast_fusion
  533.0 3.4 reshape.547
  536.4 2.8 copy.44
  539.2 2.5 convert_element_type.93
  541.7 12.0 %convert_element_type.94 = f32[1024,4096]{1,0:T(8,128)} convert(bf16[1024,4096]{1,0:T(8,128)(2,1)} %get-tuple-element.37) | non-fusion elementwise | flops 4194304 | bytes 25165824 | tf_op jit(solution)/shard_map/convert_element_type | solution.py:1243
  553.7 1.4 copy.54
  (33 shorter events, 9.6 us)
Async XLA Ops:
  536.4 2.8 copy-start.1
  541.7 12.0 %copy-start = (bf16[1152,1024]{1,0:T(8,128)(2,1)S(1)}, bf16[1152,1024]{1,0:T(8,128)(2,1)}, u32[]{:S(2)}) copy-start(bf16[1152,1024]{1,0:T(8,128)(2,1)} %get-tuple-element.33) | copy-start | bytes 7077892

commit v3 on v2

--- a/solution.py
+++ b/solution.py
@@ -24,6 +24,9 @@
         self.c = lax.rem(d, 2)
         self.x = d // 2
         self.q = self.x * nrow + self.r
+        self.qx = (1 - self.x) * nrow + self.r
+        self.qy = self.x * nrow + (1 - self.r)
+        self.qd = (1 - self.x) * nrow + (1 - self.r)
 
     def at(self, q=None, c=None, k=None):
         q = self.q if q is None else q
@@ -59,6 +62,7 @@
     def copy(self, src, dst, peer):
         at = self.used
         self.used += 1
+        assert self.used <= self.send.shape[0]
         return pltpu.make_async_remote_copy(
             src_ref=src, dst_ref=dst, send_sem=self.send.at[at], recv_sem=self.recv.at[at],
             device_id=peer, device_id_type=MESH,
@@ -79,6 +83,69 @@
 def sent_all(copies):
     for copy in copies:
         copy.wait_send()
+
+
+class Spread:
+    def __init__(self, me, links, strip):
+        self.me, self.links, self.strip = me, links, strip
+        self.first = self.second = ()
+
+    def start(self):
+        me = self.me
+        own = self.strip(me.q, None)
+        self.first = start_all([self.links.copy(own, own, me.at(q=q)) for q in (me.qx, me.qy)])
+
+    def pass_on(self):
+        me = self.me
+        along_y = self.strip(me.qx, 0)
+        along_x = self.strip(me.qy, 1)
+        self.second = [
+            self.links.copy(along_y, along_y, me.at(q=me.qy)),
+            self.links.copy(along_x, along_x, me.at(q=me.qx)),
+        ]
+        for arrived, copy in zip(self.first, self.second):
+            arrived.wait_recv()
+            copy.start()
+
+    def finish(self):
+        recv_all(self.second)
+
+    def sent(self):
+        sent_all(self.first)
+        sent_all(self.second)
+
+
+class Gather:
+    def __init__(self, me, links, chunk, slot):
+        self.me, self.links, self.chunk, self.slot = me, links, chunk, slot
+        self.early = [[], []]
+        self.late = [None, None]
+
+    def start(self, half):
+        me = self.me
+        to = me.qx if half == 0 else me.qy
+        self.early[half] = start_all([
+            self.links.copy(self.chunk(q, half), self.slot(i, half), me.at(q=to)) for i, q in ((1, me.qd), (0, to))
+        ])
+
+    def passing(self, half):
+        self.early[half][0].wait_recv()
+        return self.me.qy if half == 0 else self.me.qx
+
+    def pass_on(self, half, total):
+        to = self.me.qy if half == 0 else self.me.qx
+        self.late[half] = self.links.copy(total, self.slot(2, half), self.me.at(q=to))
+        self.late[half].start()
+
+    def finish(self):
+        for half in range(2):
+            self.early[half][1].wait_recv()
+            self.late[half].wait_recv()
+
+    def sent(self):
+        for half in range(2):
+            sent_all(self.early[half])
+            self.late[half].wait_send()
 
 
 def rows_of(start, size, unit):
@@ -357,16 +424,22 @@
     bias[0] = bias_part[...]
     column_masks(cmask, zero.width)
 
-    def across(weights, row, arrived):
-        recv_all(arrived)
-        part = weights.at[pl.ds(1, nz - 1), row]
-        return start_all([links.copy(part, part, me.at(q=me.chip(t))) for t in range(1, me.nq)])
-
-    def between_cores(weights, height, arrived):
-        recv_all(arrived)
+    def strips(weights, height):
+        wide = weights.shape[2]
+
+        def strip(q, half):
+            rows = rows_of((me.c * me.nq + q) * height, height, height)
+            cols = pl.ds(0, wide) if half is None else pl.ds(half * (wide // 2), wide // 2)
+            return weights.at[pl.ds(1, nz - 1), rows, cols]
+
+        return Spread(me, links, strip)
+
+    def between_cores(weights, height):
         half = rows_of(me.c * (me.nq * height), me.nq * height, height)
         part = weights.at[pl.ds(1, nz - 1), half]
         return start_all([links.copy(part, part, me.at(c=1 - me.c))])
+
+    pa, pb = strips(rin, ra), strips(rout, rb)
 
     first = (1 - me.r).astype(F32)
     neighbour = me.at(q=me.x * nrow + (nrow - 1 - me.r))
@@ -381,7 +454,8 @@
     head_stage(zero, 1, masked, s2.at[0], gains.at[0], biases.at[0], mask_zero, hid.at[0], hid.at[1], edge_zero, first)
     rim0 = links.copy(edge_zero, rim_zero, neighbour)
     rim0.start()
-    pa = across(rin, row_a, za)
+    recv_all(za)
+    pa.start()
     rim0.wait_recv()
     depth_stage(zero, hid.at[1], rim_zero, taps.at[0], cmask, hid.at[2], first, C)
     for copy in convs[1:]:
@@ -390,16 +464,20 @@
     def to_pooled(i, rows, out):
         mg[1, one.rows(i)] = nn(pool[i], out.astype(BF)).astype(BF)
 
+    pa.pass_on()
     tail_stage(zero, 1, mg.at[0], s2.at[1], gains.at[0], biases.at[0], mask_zero, hid.at[2], hid.at[3], to_pooled)
     kept_zero = pltpu.make_async_copy(hid, keep_zero, local.at[2])
     kept_zero.start()
+    recv_all(zb)
+    pb.start()
+    pa.finish()
+    ca = between_cores(rin, ra)
     all_one = one.cells * one.count
     part = [mg.at[1 + i // 3, pl.ds((i % 3) * all_one, all_one)] for i in range(5)]
     pooled, pre_one, hidden, pre_two, pre_three = part
     head_stage(one, one.count, lambda rows: pooled[rows], s2.at[2], gains.at[1], biases.at[1], mask_one, pre_one, hidden, edge_one, first)
     rim1 = links.copy(edge_one, rim_one, neighbour)
     rim1.start()
-    pb = across(rout, row_b, zb)
     rim1.wait_recv()
     depth_stage(one, hidden, rim_one, taps.at[1], None, pre_two, first, C)
     here = rows_of(me.k * T, T, 16)
@@ -413,13 +491,11 @@
     zg = start_all([
         links.copy(abst.at[here], abst.at[here], me.at(k=lax.rem(me.k + nz - t, nz))) for t in range(1, nz)
     ])
-    ca = between_cores(rin, ra, pa)
-    cb = between_cores(rout, rb, pb)
+    pb.pass_on()
     for copy in own + [kept_zero, kept_one]:
         copy.wait()
     recv_all(zc)
     recv_all(ca)
-    recv_all(cb)
 
     hsum[...] = jnp.zeros_like(hsum)
     ag = [None] + [
@@ -427,27 +503,89 @@
     ]
     NT = min(512, hw)
 
-    def group(t):
-        z = me.deep(t)
-        rows = rows_of(z * T, T, 16)
-
-        def unit(i, carry):
+    def hidden_group(t):
+        rows = rows_of(me.deep(t) * T, T, 16)
+
+        def front(i, carry):
             u = i // (hw // NT)
             cols = rows_of(lax.rem(i, hw // NT) * NT, NT, 128)
-            pre = nn(abst[rows], rin[u, :, cols]) + bias[u, 0:1, cols]
-            up = nt(cot[rows], rout[u, cols, :])
-            value, slope = gelu_pair(pre)
+            value, slope = gelu_pair(nn(abst[rows], rin[u, :, cols]) + bias[u, 0:1, cols])
             hid[u, rows, cols] = value.astype(BF)
-            grad = (up * slope).astype(BF)
-            mg[u, rows, cols] = grad
-            hsum[me.deep(u), 0:1, cols] += jnp.sum(grad.astype(F32), axis=0, keepdims=True)
+            mg[u, rows, cols] = slope.astype(BF)
             return carry
 
-        lax.fori_loop(0, nz * (hw // NT), unit, 0)
-        CT = 256
+        lax.fori_loop(0, nz * (hw // NT), front, 0)
+
+    for t in range(nz):
+        if t:
+            zg[t - 1].wait_recv()
+        hidden_group(t)
+        if t == 1:
+            pb.finish()
+            cb = between_cores(rout, rb)
+
+    HT = 256
+
+    def g2(i, carry):
+        u = i // (hw // HT)
+        at = rows_of(lax.rem(i, hw // HT) * HT, HT, HT)
+        s2[me.deep(u), at, :] = tn(hid[u, :, at], cot[...]).astype(BF)
+        return carry
+
+    lax.fori_loop(0, nz * (hw // HT), g2, 0)
+    half = me.nq * rb
+    theirs = rows_of((1 - me.c) * half, half, half)
+    core2 = start_all([links.copy(s2.at[:, theirs], rc2, me.at(c=1 - me.c))])
+    abst_t[...] = abst[...].T
+    recv_all(cb)
+
+    def unit(i, carry):
+        u = i // (hw // 256)
+        cols = rows_of(lax.rem(i, hw // 256) * 256, 256, 256)
+        grad = (nt(cot[...], rout[u, cols, :]) * mg[u, :, cols].astype(F32)).astype(BF)
+        mg[u, :, cols] = grad
+        hsum[me.deep(u), 0:1, cols] += jnp.sum(grad.astype(F32), axis=0, keepdims=True)
+        return carry
+
+    lax.fori_loop(0, nz * (hw // 256), unit, 0)
+
+    recv_all(core2)
+    mine2 = me.c * half
+    gather2 = Gather(
+        me, links,
+        lambda q, h: s2.at[pl.ds(h * (nz // 2), nz // 2), rows_of(mine2 + q * rb, rb, rb)],
+        lambda i, h: rp2.at[i, pl.ds(h * (nz // 2), nz // 2)],
+    )
+    piece = 256
+    parts = half // piece
+    loads = [
+        pltpu.make_async_copy(
+            rc2.at[i // parts, pl.ds(i % parts * piece, piece)], ag_send.at[i % 2, pl.ds(0, piece)], local.at[i % 2]
+        )
+        for i in range(nz * parts)
+    ]
+    loads[0].start()
+    for i in range(nz * parts):
+        loads[i].wait()
+        if i + 1 < nz * parts:
+            loads[i + 1].start()
+        j, where = i // parts, mine2 + i % parts * piece
+        fold(
+            lambda at, v, j=j, w=where: s2.__setitem__((j, rows_of(w + at.start, at.size, 16)), v.astype(BF)),
+            [
+                lambda at, j=j, w=where: s2[j, rows_of(w + at.start, at.size, 16)],
+                lambda at, i=i: ag_send[i % 2, at],
+            ],
+            piece, 32,
+        )
+        if (i + 1) % (nz // 2 * parts) == 0:
+            gather2.start(i // (nz // 2 * parts))
+
+    def group_back(t):
+        rows = rows_of(me.deep(t) * T, T, 16)
 
         def back(i, carry):
-            at = rows_of(i * CT, CT, CT)
+            at = rows_of(i * 256, 256, 256)
             total = nt(mg[0, rows, :], rin[0, at, :])
             for u in range(1, nz):
                 total = total + nt(mg[u, rows, :], rin[u, at, :])
@@ -457,29 +595,44 @@
                 ag_send[t - 1, :, at] = total.astype(BF)
             return carry
 
-        lax.fori_loop(0, C // CT, back, 0)
-
-    for t in range(nz):
-        if t:
-            zg[t - 1].wait_recv()
-        group(t)
+        lax.fori_loop(0, C // 256, back, 0)
         if t:
             ag[t].start()
 
-    HT = 256
-
-    def g2(i, carry):
-        u = i // (hw // HT)
-        at = rows_of(lax.rem(i, hw // HT) * HT, HT, HT)
-        s2[me.deep(u), at, :] = tn(hid[u, :, at], cot[...]).astype(BF)
+    for t in (*range(1, nz), 0):
+        group_back(t)
+
+
+    sent_all(ca)
+    pa.sent()
+
+    def g1(i, carry):
+        u = i // (C // 256)
+        at = rows_of(lax.rem(i, C // 256) * 256, 256, 256)
+        rin[u, at, :] = nn(abst_t[at, :], mg[u]).astype(BF)
         return carry
 
-    lax.fori_loop(0, nz * (hw // HT), g2, 0)
-    half = me.nq * rb
-    theirs = rows_of((1 - me.c) * half, half, half)
-    core2 = start_all([links.copy(s2.at[:, theirs], rc2, me.at(c=1 - me.c))])
-
-    abst_t[...] = abst[...].T
+    lax.fori_loop(0, nz * (C // 256), g1, 0)
+    low = me.nq * ra
+    core1 = links.copy(rin.at[:, rows_of((1 - me.c) * low, low, low)], rc1, me.at(c=1 - me.c))
+    core1.start()
+
+    for h in range(2):
+        to = gather2.passing(h)
+        block = range(h * (nz // 2), (h + 1) * (nz // 2))
+        loads = [pltpu.make_async_copy(rp2.at[1, j], mg.at[j, pl.ds(0, rb)], local.at[j]) for j in block]
+        for copy in loads:
+            copy.start()
+        for j, copy in zip(block, loads):
+            copy.wait()
+            where = mine2 + to * rb
+            fold(
+                lambda at, v, j=j, w=where: s2.__setitem__((j, rows_of(w + at.start, at.size, 16)), v.astype(BF)),
+                [lambda at, j=j, w=where: s2[j, rows_of(w + at.start, at.size, 16)], lambda at, j=j: mg[j, at]],
+                rb, min(rb, 32),
+            )
+        gather2.pass_on(h, gather2.chunk(to, h))
+
     sent_all(zg)
 
     def f2_body(i, carry):
@@ -493,38 +646,6 @@
     lax.fori_loop(0, ow // 256, f2_body, 0)
     out_tokens = pltpu.make_async_copy(abst, tokens, local.at[6])
     out_tokens.start()
-    recv_all(core2)
-    sent_all(core2)
-    loads = [
-        pltpu.make_async_copy(rc2.at[j], hid.at[j, pl.ds(0, half)], local.at[j]) for j in range(nz)
-    ]
-    for copy in loads:
-        copy.start()
-    for j in range(nz):
-        loads[j].wait()
-        fold(
-            lambda at, v, j=j: s2.__setitem__((j, rows_of(me.c * half + at.start, at.size, 16)), v.astype(BF)),
-            [lambda at, j=j: s2[j, rows_of(me.c * half + at.start, at.size, 16)], lambda at, j=j: hid[j, at]],
-            half, 32,
-        )
-    sends2 = []
-    for t in range(1, me.nq):
-        q = me.chip(t)
-        src = s2.at[:, rows_of((me.c * me.nq + q) * rb, rb, rb)]
-        sends2.append(links.copy(src, rp2.at[t - 1], me.at(q=q)))
-    start_all(sends2)
-
-
-    def g1(i, carry):
-        u = i // (C // 256)
-        at = rows_of(lax.rem(i, C // 256) * 256, 256, 256)
-        hid[u, at, :] = nn(abst_t[at, :], mg[u]).astype(BF)
-        return carry
-
-    lax.fori_loop(0, nz * (C // 256), g1, 0)
-    low = me.nq * ra
-    core1 = links.copy(hid.at[:, rows_of((1 - me.c) * low, low, low)], rc1, me.at(c=1 - me.c))
-    core1.start()
     recv_all(ag[1:])
     fold(
         lambda at, v: agrad.__setitem__(at, v),
@@ -539,18 +660,17 @@
     for u in range(nz):
         loads[u].wait()
         fold(
-            lambda at, v, u=u: hid.__setitem__((u, rows_of(me.c * low + at.start, at.size, 16)), v.astype(BF)),
-            [lambda at, u=u: hid[u, rows_of(me.c * low + at.start, at.size, 16)], lambda at, u=u: mg[u, at]],
+            lambda at, v, u=u: rin.__setitem__((u, rows_of(me.c * low + at.start, at.size, 16)), v.astype(BF)),
+            [lambda at, u=u: rin[u, rows_of(me.c * low + at.start, at.size, 16)], lambda at, u=u: mg[u, at]],
             low, 32,
         )
-        outs.append(pltpu.make_async_copy(hid.at[u, rows_of(me.c * low, low, low)], s1.at[u], local.at[u]))
+        outs.append(pltpu.make_async_copy(rin.at[u, rows_of(me.c * low, low, low)], s1.at[u], local.at[u]))
         outs[-1].start()
+    gather2.finish()
     for copy in outs:
         copy.wait()
-    recv_all(sends2)
     loads = [
-        pltpu.make_async_copy(rp2.at[t - 1], mg.at[pl.ds(0, nz), pl.ds(t * rb, rb)], local.at[t - 1])
-        for t in range(1, me.nq)
+        pltpu.make_async_copy(rp2.at[i], mg.at[pl.ds(0, nz), pl.ds(i * rb, rb)], local.at[i]) for i in (0, 2)
     ]
     for copy in loads:
         copy.start()
@@ -560,11 +680,13 @@
         fold(
             lambda at, v, j=j: f2.__setitem__((j, at), v.astype(BF)),
             [lambda at, j=j: s2[j, rows_of(strip * rb + at.start, at.size, 16)]]
-            + [lambda at, j=j, t=t: mg[j, rows_of(t * rb + at.start, at.size, 16)] for t in range(1, me.nq)],
+            + [lambda at, j=j, i=i: mg[j, rows_of(i * rb + at.start, at.size, 16)] for i in (0, 2)],
             rb, min(rb, 32),
         )
     out_tokens.wait()
-    for group_of in (za, zb, zc, pa, pb, ca, cb, ag[1:], sends2, [rim0, rim1, core1]):
+    for group in (pb, gather2):
+        group.sent()
+    for group_of in (za, zb, zc, cb, core2, ag[1:], [rim0, rim1, core1]):
         sent_all(group_of)
 
 
@@ -574,7 +696,7 @@
     mask_zero, mask_one, pool, pick, small_in,
     out1, out2, out3, small, patch_grad, rp1,
     xs, kept, keep, third, resid, weights, cmask, edge_zero, edge_one, got_zero, got_one,
-    f1, rz1, conv, rc3, rp3, f3, rz3, sc, sp, sz, send, recv, local,
+    sent_on, f1, rz1, conv, rc3, rp3, f3, rz3, sc, sp, sz, send, recv, local,
 ):
     me = Place(nz, ndp, nrow)
     links = Links(send, recv)
@@ -599,10 +721,14 @@
     ]
     for copy in loads:
         copy.start()
-    p1 = start_all([
-        links.copy(s1.at[:, rows_of(me.chip(t) * ra, ra, ra)], rp1.at[t - 1], me.at(q=me.chip(t)))
-        for t in range(1, me.nq)
-    ])
+    lead = nz // 2
+    gather1 = Gather(
+        me, links,
+        lambda q, h: s1.at[pl.ds(h * lead, lead), rows_of(q * ra, ra, ra)],
+        lambda i, h: rp1.at[i, pl.ds(h * lead, lead)],
+    )
+    gather1.start(0)
+    gather1.start(1)
     row_b = rows_of(strip * rb, rb, rb)
     col_k = rows_of(me.k * ow, ow, 128)
     z2 = start_all([
@@ -623,12 +749,26 @@
                     [lambda at, i=(b, m, x, me.c): conv[(*i, at)], lambda at, i=(b, m, x): rc3[(*i, at)]],
                     nz * R, 32,
                 )
-        sends = []
-        for t in range(1, me.nq):
-            q = me.chip(t)
-            cols = rows_of(lax.rem(q, nrow) * width, width, 128)
-            sends.append(links.copy(conv.at[b, :, q // nrow, me.c, :, cols], rp3.at[b, t - 1], me.at(q=q)))
-        return start_all(sends)
+        gather = Gather(
+            me, links,
+            lambda q, h: conv.at[b, h, q // nrow, me.c, :, rows_of(lax.rem(q, nrow) * width, width, 128)],
+            lambda i, h: rp3.at[b, i, h],
+        )
+        gather.start(1)
+        gather.start(0)
+        return gather
+
+    def spread_on(b):
+        for h in (1, 0):
+            to = p3[b].passing(h)
+            cols = rows_of(lax.rem(to, nrow) * width, width, 128)
+            x = to // nrow
+            fold(
+                lambda at, v: conv.__setitem__((b, h, x, me.c, at, cols), v.astype(BF)),
+                [lambda at: conv[b, h, x, me.c, at, cols], lambda at: rp3[b, 1, h, at, :]],
+                nz * R, 32,
+            )
+            p3[b].pass_on(h, p3[b].chunk(to, h))
 
     core3, p3 = [None, None], [None, None]
 
@@ -677,9 +817,51 @@
     rim0 = links.copy(edge_zero, got_zero, neighbour)
     rim0.start()
     p3[1] = spread(1)
+    temp = [keep.at[0, pl.ds(i * lead * ra, lead * ra)] for i in range(4)]
+
+    def bring(sources):
+        copies = [
+            pltpu.make_async_copy(source.at[j], to.at[pl.ds(j * ra, ra)], local.at[6 + n * lead + j])
+            for n, (source, to) in enumerate(sources)
+            for j in range(lead)
+        ]
+        for copy in copies:
+            copy.start()
+        for copy in copies:
+            copy.wait()
+
+    for h in range(2):
+        to = gather1.passing(h)
+        bring([(gather1.chunk(to, h), temp[2 * h]), (gather1.slot(1, h), temp[2 * h + 1])])
+        for j in range(lead):
+            fold(
+                lambda at, v: sent_on.__setitem__((h, j, at), v.astype(BF)),
+                [lambda at, ref=ref: ref[rows_of(j * ra + at.start, at.size, 16)] for ref in temp[2 * h : 2 * h + 2]],
+                ra, 32,
+            )
+        gather1.pass_on(h, sent_on.at[h])
     outer_stage(third, kept.at[3], conv.at[0, 1])
     rim0.wait_recv()
+    own2.wait()
+    recv_all(z2)
+    spread2 = Spread(me, links, lambda q, h: out2.at[
+        rows_of((me.c * me.nq + q) * rb, rb, rb),
+        pl.ds(0, nz * ow) if h is None else pl.ds(h * (nz * ow // 2), nz * ow // 2),
+    ])
+    spread2.start()
     back_depth_stage(zero, kept.at[2], got_zero, kept.at[1], rim_zero, taps.at[0], cmask, third, first, C, small, 0)
+    spread_on(1)
+    gather1.finish()
+    for h in range(2):
+        mine = [keep.at[0, pl.ds(i * lead * ra, lead * ra)] for i in range(3)]
+        bring([(gather1.chunk(me.q, h), mine[0]), (gather1.slot(0, h), mine[1]), (gather1.slot(2, h), mine[2])])
+        for j in range(lead):
+            fold(
+                lambda at, v: f1.__setitem__((h * lead + j, at), v.astype(BF)),
+                [lambda at, ref=ref: ref[rows_of(j * ra + at.start, at.size, 16)] for ref in mine],
+                ra, 32,
+            )
+    z1 = start_all([links.copy(f1.at[t], rz1.at[t - 1], me.at(k=me.deep(t))) for t in range(1, nz)])
     again[1].wait()
 
     def to_patches(i, rows, grad):
@@ -696,56 +878,7 @@
     sums = start_all([links.copy(small, sc, other)])
     p3[0] = spread(0)
 
-    own2.wait()
-    recv_all(z2)
-    g2 = start_all([
-        links.copy(out2.at[row_b], out2.at[row_b], me.at(q=me.chip(t))) for t in range(1, me.nq)
-    ])
-    recv_all(sums)
-    sent_all(sums)
-    small[...] += sc[...]
-    sums_p = start_all([links.copy(small, sp.at[t - 1], me.at(q=me.chip(t))) for t in range(1, me.nq)])
-
-    recv_all(p1)
-    pieces = [
-        pltpu.make_async_copy(
-            (s1.at[j, rows_of(me.q * ra, ra, ra)] if t == 0 else rp1.at[t - 1, j]), kept.at[t, pl.ds(j * ra, ra)], local.at[6 + t * nz + j]
-        )
-        for t in range(me.nq)
-        for j in range(nz)
-    ]
-    for copy in pieces:
-        copy.start()
-    for copy in pieces:
-        copy.wait()
-    for j in range(nz):
-        fold(
-            lambda at, v, j=j: f1.__setitem__((j, at), v.astype(BF)),
-            [lambda at, j=j, t=t: kept[t, rows_of(j * ra + at.start, at.size, 16)] for t in range(me.nq)],
-            ra, 32,
-        )
-    z1 = start_all([links.copy(f1.at[t], rz1.at[t - 1], me.at(k=me.deep(t))) for t in range(1, nz)])
-    z3 = [None, None]
-    my_cols = rows_of(me.r * width, width, 128)
-    for b in (1, 0):
-        recv_all(p3[b])
-        for m in range(2):
-            for j in range(nz):
-                rows = pl.ds(j * R, R)
-                total = conv[b, m, me.x, me.c, rows, my_cols].astype(F32)
-                for t in range(1, me.nq):
-                    total = total + rp3[b, t - 1, m, rows, :].astype(F32)
-                f3[b, j, pl.ds(m * R, R)] = total.astype(BF)
-        z3[b] = start_all([
-            links.copy(f3.at[b, me.deep(t)], rz3.at[b, t - 1], me.at(k=me.deep(t))) for t in range(1, nz)
-        ])
-
-    sent_all(sums_p)
-    recv_all(sums_p)
-    for t in range(1, me.nq):
-        small[...] += sp[t - 1]
-    sums_z = start_all([links.copy(small, sz.at[t - 1], me.at(k=me.deep(t))) for t in range(1, nz)])
-
+    spread2.pass_on()
     recv_all(z1)
     row_a = rows_of(strip * ra, ra, ra)
     fold(
@@ -753,9 +886,41 @@
         [lambda at: f1[0, at]] + [lambda at, t=t: rz1[t - 1, at] for t in range(1, nz)],
         ra, 32,
     )
-    g1 = start_all([
-        links.copy(out1.at[row_a], out1.at[row_a], me.at(q=me.chip(t))) for t in range(1, me.nq)
+    spread1 = Spread(me, links, lambda q, h: out1.at[
+        rows_of((me.c * me.nq + q) * ra, ra, ra), pl.ds(0, hw) if h is None else pl.ds(h * (hw // 2), hw // 2)
     ])
+    spread1.start()
+    recv_all(sums)
+    sent_all(sums)
+    small[...] += sc[...]
+    sums_p = start_all([links.copy(small, sp.at[t - 1], me.at(q=me.chip(t))) for t in range(1, me.nq)])
+
+    spread_on(0)
+    z3 = [None, None]
+    my_cols = rows_of(me.r * width, width, 128)
+
+    def deepen(b):
+        p3[b].finish()
+        for m in range(2):
+            for j in range(nz):
+                rows = pl.ds(j * R, R)
+                total = conv[b, m, me.x, me.c, rows, my_cols].astype(F32)
+                for i in (0, 2):
+                    total = total + rp3[b, i, m, rows, :].astype(F32)
+                f3[b, j, pl.ds(m * R, R)] = total.astype(BF)
+        z3[b] = start_all([
+            links.copy(f3.at[b, me.deep(t)], rz3.at[b, t - 1], me.at(k=me.deep(t))) for t in range(1, nz)
+        ])
+
+    deepen(1)
+    spread1.pass_on()
+    sent_all(sums_p)
+    recv_all(sums_p)
+    for t in range(1, me.nq):
+        small[...] += sp[t - 1]
+    sums_z = start_all([links.copy(small, sz.at[t - 1], me.at(k=me.deep(t))) for t in range(1, nz)])
+    deepen(0)
+
     g3 = []
     for b in (1, 0):
         recv_all(z3[b])
@@ -767,10 +932,10 @@
             links.copy(out3.at[b, me.r], out3.at[b, me.r], me.at(q=me.x * nrow + lax.rem(me.r + t, nrow)))
             for t in range(1, nrow)
         ])
-    recv_all(g2)
+    spread2.finish()
     half_b = rows_of(me.c * me.nq * rb, me.nq * rb, me.nq * rb)
     h2 = start_all([links.copy(out2.at[half_b], out2.at[half_b], other)])
-    recv_all(g1)
+    spread1.finish()
     half_a = rows_of(me.c * me.nq * ra, me.nq * ra, me.nq * ra)
     h1 = start_all([links.copy(out1.at[half_a], out1.at[half_a], other)])
     sent_all(sums_z)
@@ -781,8 +946,10 @@
     recv_all(h1)
     recv_all(h2)
     out_patches.wait()
-    for group_of in (core3, z2, p1, p3[0], p3[1], g2, z1, z3[0], z3[1], g1, g3, h1, h2, [rim0, rim1]):
+    for group_of in (core3, z2, z1, z3[0], z3[1], g3, h1, h2, [rim0, rim1]):
         sent_all(group_of)
+    for group in (gather1, p3[0], p3[1], spread1, spread2):
+        group.sent()
 
 
 def spec(*kinds):
@@ -796,7 +963,7 @@
     hw, ow = read_out.shape[0], cot.shape[1]
     tall = nz * T
     rb = hw // (2 * nq)
-    copies = 4 * (nz - 1) + 2 * (nq - 1) + 2 + (nz - 1) + 1 + (nq - 1) + 3
+    copies = 5 * (nz - 1) + 24
     bias_part = jnp.broadcast_to(read_bias[0:1], (8, hw))
     bias_out = jnp.broadcast_to(read_bias[1:2], (8, ow))
     ANY = pl.ANY
@@ -856,7 +1023,7 @@
     R = C // (ndp * nz)
     tall = patches.shape[0]
     S = 40
-    copies = 1 + 2 + (nz - 1) + (nq - 1) * 2 + 2 * (nq - 1) + (nq - 1) + (nz - 1) * 2 + 2 * (nz - 1) + (nq - 1) + 2 * (nrow - 1) + 2 + 2
+    copies = 5 * (nz - 1) + 40
     width = C // nrow
     ANY = pl.ANY
     return pl.pallas_call(
@@ -883,6 +1050,7 @@
             VMEM((one.count, 16, C), BF),
             VMEM((zero.count, 32, C), BF),
             VMEM((one.count, 16, C), BF),
+            VMEM((2, nz // 2, ra, hw), BF),
             VMEM((nz, ra, hw), BF),
             VMEM((nz - 1, ra, hw), BF),
             VMEM((2, 2, nx, 2, nz * R, C), BF),

time: 565 us -> 493 us (0.87)
  the two profiles are of different devices: /device:TPU:17 before, /device:TPU:11 now
where the time goes in v3:
time: 493 us; the launch traced here: 483 us
  Pallas kernels  428 us (87%)
  local copies, waits for them, and re-layouts  28.4 us (6%)
  other arithmetic  25.6 us (5%)
    pallas_call x1, Pallas kernels, run_readout(): pl.pallas_call(functools.partial(readout_kernel, nz, ndp, nrow, zero, one...  240 us
    pallas_call x1, Pallas kernels, run_grads(): pl.pallas_call(functools.partial(grads_kernel, nz, ndp, nrow, zero, one),...  188 us
    unnamed x13, local copies, waits for them, and re-layouts  12.4 us
    convert_element_type x1, other arithmetic, on_device(): out2.astype(F32)  12 us

profile of v3, /device:TPU:11, one launch (start us, length us, event | category | flops | bytes accessed | tf_op | source)
XLA Modules:
  0.0 482.8 jit_solution(15521335488861322423)
XLA Ops:
  2.2 2.1 convert_reduce_fusion
  5.9 0.8 fusion.25
  8.4 1.4 copy.34.gains
  9.8 1.4 copy.35.biases
  11.1 1.4 copy_convert_fusion.taps
  13.2 0.8 fusion.1.pick
  14.0 0.8 fusion.pick
  14.8 1.0 reshape.556.mask_zero
  16.2 2.1 convert_element_type.85.pool
  18.3 3.0 copy.32
  21.3 2.1 reshape.546.cot
  23.4 239.6 %readout.1 = (bf16[1152,1024]{1,0:T(8,128)(2,1)}, f32[288,1024]{1,0:T(8,128)}, bf16[4,512,1024]{2,1,0:T(8,128)(2,1)}, bf16[4,128,1024]{2,1,0:T(8,128)(2,1)}, f32...) custom-call(bf16[1152,1024]{1,0:T(8,128)(2,1)} %bitcast.19, ...), custom_call_target="tpu_custom_call" | custom-call | tf_op jit(solution)/shard_map/readout/pallas_call | solution.py:970
  264.4 187.9 %grads.1 = (bf16[1024,1024]{1,0:T(8,128)(2,1)}, bf16[1024,4096]{1,0:T(8,128)(2,1)}, bf16[2,2,128,512]{3,2,1,0:T(8,128)(2,1)}, f32[40,1024]{1,0:T(8,128)}, bf16[1...) custom-call(bf16[4,512,1024]{2,1,0:T(8,128)(2,1)} %get-tuple-element.25.s1, ...), custom_call_target="tpu_custom_call" | custom-call | tf_op jit(solution)/shard_map/grads/pallas_call | solution.py:1029
  452.4 0.8 constant_dynamic-slice_fusion.1
  453.2 0.8 slice.35
  456.3 1.2 convert_bitcast_fusion
  457.5 0.8 copy.40
  458.3 0.9 reshape.554
  459.2 1.0 slice_bitcast_fusion
  460.3 3.4 reshape.547
  463.7 2.8 copy.44
  466.5 2.5 convert_element_type.93
  469.0 12.0 %convert_element_type.94 = f32[1024,4096]{1,0:T(8,128)} convert(bf16[1024,4096]{1,0:T(8,128)(2,1)} %get-tuple-element.37) | non-fusion elementwise | flops 4194304 | bytes 25165824 | tf_op jit(solution)/shard_map/convert_element_type | solution.py:1411
  481.0 1.4 copy.54
  (33 shorter events, 9.6 us)
Async XLA Ops:
  463.7 2.8 copy-start.1
  469.0 12.0 %copy-start = (bf16[1152,1024]{1,0:T(8,128)(2,1)S(1)}, bf16[1152,1024]{1,0:T(8,128)(2,1)}, u32[]{:S(2)}) copy-start(bf16[1152,1024]{1,0:T(8,128)(2,1)} %get-tuple-element.33) | copy-start | bytes 7077892
